TPU v7x, 768 devices: a whole 4x8x12 slice. The times are simulated.
768 devices in a mesh: src: 12 (over z), freq: 2 (over y_hi), space: 32 (over x, y_lo, core).
Axes of the slice: x: 4, y: 8 (y_hi: 2, y_lo: 4; y = y_hi * 4 + y_lo), z: 12, core: 2. Of those that a mesh axis runs over, the one named last changes fastest.
Arguments:
- forward_field: float32 [12, 16, 2, 64, 3072], P('src', 'freq', None, 'space'), may hold values from -6 to 6
- adjoint_field: float32 [12, 16, 2, 64, 3072], P('src', 'freq', None, 'space'), may hold values from -6 to 6
- source_group: int32 [12], P('src'), may hold values from 0 to 2, as said below
- group_weight: float32 [3], replicated, may hold values from 0.5 to 2
- frequency_index: int32 [16], replicated, may hold values from 0 to 15, each once
- log_sigma: float32 [64, 3072], P('space', ('src', 'freq')), may hold values from -1 to 1
- charge: float32 [64, 3072], P('space', ('src', 'freq')), may hold values from 0.05 to 0.6
- log_tau: float32 [64, 3072], P('space', ('src', 'freq')), may hold values from -6.9 to 0
- exponent: float32 [64, 3072], P('space', ('src', 'freq')), may hold values from 0.2 to 0.8
- active: int32 [64, 3072], P('space', ('src', 'freq')), may hold values 0 or 1
- prior_weight: float32 [4, 3], replicated, may hold values from 0.03 to 0.15
Outputs:
- smoothed: float32 [4, 64, 3072], P(None, 'space', ('src', 'freq'))
Inputs may be any that keep to these rules, and one draw needn't show every extreme that they name: `source_group`: every one of the 3 groups holds at least one source. `frequency_index`: A permutation of the frequency list positions.
All inputs are finite; a program needn't handle non-finite values. No bound on the sum of `active` on one device may be relied on, other than what follows from the above.
Results may differ from a plain program's by a relative error of at most 0.0002.
Values sent between devices are 32-bit elements; how exact they have to be, the bound alone decides.
A program may use at most 64 MiB of HBM per device.

v0:
```python
import math

import jax
import jax.numpy as jnp
from jax import lax
from jax.sharding import PartitionSpec as P

FREQ = 16
GROUPS = 3
NY = 64


def padded_2(x, sides, width):
    for axis, dim in sides:
        size, length = (lax.axis_size(axis), x.shape[dim])
        up = [(i, (i + 1) % size) for i in range(size - 1)]
        down = [(j, i) for i, j in up]
        last = lax.slice_in_dim(x, length - width, length, axis=dim)
        initial = lax.slice_in_dim(x, 0, width, axis=dim)
        before = lax.ppermute(last, axis, up)
        after = lax.ppermute(initial, axis, down)
        x = jnp.concatenate([before, x, after], axis=dim)
    return x


def gradients(extended, y_cells):
    grad_x = 0.5 * (extended[..., 2:, :] - extended[..., :-2, :])
    centre = extended[..., 1:-1, :]
    cells = centre.shape[-1]
    z_padding = [(0, 0)] * (centre.ndim - 1) + [(y_cells, y_cells)]
    padded = jnp.pad(centre, z_padding)
    grad_z = 0.5 * (padded[..., 2 * y_cells :] - padded[..., :cells])
    y_padding = [(0, 0)] * (centre.ndim - 1) + [(1, 1)]
    padded = jnp.pad(centre, y_padding)
    y_pos = jnp.arange(cells, dtype=jnp.int32) % y_cells
    upper = jnp.where(y_pos < y_cells - 1, padded[..., 2:], 0.0)
    lower = jnp.where(y_pos > 0, padded[..., :-2], 0.0)
    grad_y = 0.5 * (upper - lower)
    return (grad_x, grad_y, grad_z)


def correlate(grad_parts):
    real_sum = 0.0
    imag_sum = 0.0
    for grad_part in grad_parts:
        forward_real = grad_part[0][:, :, 0]
        forward_imag = grad_part[0][:, :, 1]
        adjoint_real = grad_part[1][:, :, 0]
        adjoint_imag = grad_part[1][:, :, 1]
        real_sum = real_sum + forward_real * adjoint_real - forward_imag * adjoint_imag
        imag_sum = imag_sum + forward_real * adjoint_imag + forward_imag * adjoint_real
    return jnp.stack([real_sum, imag_sum], axis=2)


def freq_omega(index_list, count):
    return (
        2.0
        * math.pi
        * jnp.exp(math.log(10.0) * (-1.0 + 4.0 * index_list.astype(jnp.float32) / (count - 1)))
    )


def complex_product(left_real, left_imag, right_real, right_imag):
    return (
        left_real * right_real - left_imag * right_imag,
        left_real * right_imag + left_imag * right_real,
    )


def chain_rule(correlation, omega_list, log_sigma, charge, log_tau, exponent, scale_factor):
    omega_list = omega_list.reshape(omega_list.shape + (1,) * log_sigma.ndim)
    log_product = jnp.log(omega_list) + log_tau
    amplitude = jnp.exp(exponent * log_product)
    phase_angle = exponent * (0.5 * math.pi)
    zeta_real = amplitude * jnp.cos(phase_angle)
    zeta_imag = amplitude * jnp.sin(phase_angle)
    sigma_zero = jnp.exp(log_sigma)
    denom_real = 1.0 + (1.0 - charge) * zeta_real
    denom_imag = (1.0 - charge) * zeta_imag
    inverse = 1.0 / (denom_real * denom_real + denom_imag * denom_imag)
    recip_real = denom_real * inverse
    recip_imag = -denom_imag * inverse
    sigma_real, sigma_imag = complex_product(1.0 + zeta_real, zeta_imag, recip_real, recip_imag)
    square_real, square_imag = complex_product(recip_real, recip_imag, recip_real, recip_imag)
    numer_real, numer_imag = complex_product(1.0 + zeta_real, zeta_imag, zeta_real, zeta_imag)
    charge_real, charge_imag = complex_product(numer_real, numer_imag, square_real, square_imag)
    slope_real, slope_imag = complex_product(
        charge * square_real, charge * square_imag, zeta_real, zeta_imag
    )
    expo_real, expo_imag = complex_product(slope_real, slope_imag, log_product, 0.5 * math.pi)
    derivs = (
        (sigma_real, sigma_imag),
        (charge_real, charge_imag),
        (exponent * slope_real, exponent * slope_imag),
        (expo_real, expo_imag),
    )
    corr_real = correlation[:, 0]
    corr_imag = correlation[:, 1]
    rows_out = []
    for part_real, part_imag in derivs:
        rows_out.append(sigma_zero * jnp.sum(part_real * corr_real - part_imag * corr_imag, axis=0))
    return jnp.stack(rows_out) * scale_factor


def smooth_pass(extended, prior_weight):
    centre = extended[:, 1:-1, 1:-1, :]
    along_x = extended[:, 2:, 1:-1, :] + extended[:, :-2, 1:-1, :] - 2.0 * centre
    along_z = extended[:, 1:-1, 2:, :] + extended[:, 1:-1, :-2, :] - 2.0 * centre
    padded = jnp.pad(centre, ((0, 0), (0, 0), (0, 0), (1, 1)))
    along_y = padded[..., 2:] + padded[..., :-2] - 2.0 * centre
    weight_x = prior_weight[:, 0].reshape(-1, 1, 1, 1)
    weight_y = prior_weight[:, 1].reshape(-1, 1, 1, 1)
    weight_z = prior_weight[:, 2].reshape(-1, 1, 1, 1)
    return centre + weight_x * along_x + weight_y * along_y + weight_z * along_z


def local(
    forward_field,
    adjoint_field,
    source_group,
    group_weight,
    frequency_index,
    log_sigma,
    charge,
    log_tau,
    exponent,
    active,
    prior_weight,
):
    source_count, freq_count, _, x_rows, cell_count = forward_field.shape
    source_weight = jnp.sum(
        jnp.where(source_group[:, None] == jnp.arange(GROUPS)[None, :], group_weight[None, :], 0.0),
        axis=1,
    )
    stacked = jnp.stack([forward_field, adjoint_field])
    extended = padded_2(stacked, (("space", 4),), 1)
    correlation = correlate(gradients(extended, NY))
    partial_value = jnp.sum(source_weight.reshape(-1, 1, 1, 1, 1) * correlation, axis=0)
    scale_factor = 1.0 / math.sqrt(source_count * lax.axis_size("src") * FREQ)
    summed = lax.psum_scatter(partial_value, "src", scatter_dimension=3, tiled=True)
    regrouped = lax.all_to_all(summed, "freq", split_axis=3, concat_axis=0, tiled=True)
    omega_list = freq_omega(frequency_index, FREQ)
    gradient = chain_rule(regrouped, omega_list, log_sigma, charge, log_tau, exponent, scale_factor)
    masked = gradient * active.astype(jnp.float32)
    smooth_field = masked.reshape(4, x_rows, -1, NY)
    for step_index in range(2):
        rimmed = padded_2(smooth_field, ((("src", "freq"), 2), ("space", 1)), 1)
        smooth_field = smooth_pass(rimmed, prior_weight)
    return smooth_field.reshape(4, x_rows, -1)


def solution(mesh):
    placed = (
        P("src", "freq", None, "space", None),
        P("src", "freq", None, "space", None),
        P("src"),
        P(),
        P(),
        P("space", ("src", "freq")),
        P("space", ("src", "freq")),
        P("space", ("src", "freq")),
        P("space", ("src", "freq")),
        P("space", ("src", "freq")),
        P(),
    )
    return jax.shard_map(
        local,
        mesh=mesh,
        in_specs=placed,
        out_specs=P(None, "space", ("src", "freq")),
        check_vma=False,
    )
```

profile of v0, /device:TPU:6, one launch (start us, length us, event | category | flops | bytes accessed | tf_op | source)
XLA Modules:
  0.0 207.3 jit_solution(7554255824316583624)
XLA Ops:
  6.5 1.2 copy_bitcast_fusion
  7.7 0.6 fusion.2
  8.3 5.2 %collective-permute-start = (f32[2,1,8,2,1,3072]{5,4,2,3,1,0:T(1,128)S(1)}, f32[2,1,8,2,1,3072]{5,4,2,3,1,0:T(1,128)S(1)}, u32[]{:S(2)}, u32[]{:S(2)}) collective-permute-start(f32[2,1,8,2,1,3072]{5,4,2,3,1,0:T(1,128)S(1)} %get-tuple-element.16), channel_id=1, source_target_pairs={{1,0},{2,1},{3,2},{4,3},{5,4},{6,5},{7,6},{8,7},{9,8},{10,9},{11,1... | collective-permute-start | bytes 1179656 | tf_op jit(solution)/shard_map/ppermute | solution.py:21
  13.6 1.9 collective-permute-start.1
  16.2 0.7 fusion.65
  16.8 5.9 %collective-permute-done = f32[2,1,8,2,1,3072]{5,4,2,3,1,0:T(1,128)S(1)} collective-permute-done((f32[2,1,8,2,1,3072]{5,4,2,3,1,0:T(1,128)S(1)}, f32[2,1,8,2,1,3072]{5,4,2,3,1,0:T(1,128)S(1)}, u32[]{:S(2)}, u32[]{:S(2)}) %collective-permute-start) | collective-permute-done | bytes 393248 | tf_op jit(solution)/shard_map/ppermute | solution.py:21
  22.7 2.7 %collective-permute-done.1 = f32[2,1,8,2,1,3072]{5,4,2,3,1,0:T(1,128)S(1)} collective-permute-done((f32[2,1,8,2,1,3072]{5,4,2,3,1,0:T(1,128)S(1)}, f32[2,1,8,2,1,3072]{5,4,2,3,1,0:T(1,128)S(1)}, u32[]{:S(2)}, u32[]{:S(2)}) %collective-permute-start.1) | collective-permute-done | bytes 393248 | tf_op jit(solution)/shard_map/ppermute | solution.py:20
  25.4 1.6 fusion.1
  26.9 3.4 %subtract_multiply_fusion.1 = (f32[2,1,8,2,2,3072]{5,4,2,3,1,0:T(2,128)S(1)}, f32[2,1,8,2,2,3072]{5,4,2,3,1,0:T(2,128)S(1)}) fusion(f32[2,1,8,2,2,3072]{5,4,2,3,1,0:T(2,128)S(1)} %get-tuple-element.15, pred[3072]{0:T(1024)(128)(4,1)S(1)} %get-tuple-element.40, pred[3072]{0:T(1024)(128)(4,1)S(1)} %get-tuple-element.41), kind=kLoop, calls=%fused_computation.12 | loop fusion | flops 1179648 | bytes 2365440 | tf_op jit(solution)/shard_map/mul | solution.py:38
  30.4 0.1 slice_bitcast_fusion.3
  30.4 0.1 slice_bitcast_fusion.1
  30.5 0.5 subtract_bitcast_fusion
  31.1 0.5 add_bitcast_fusion
  31.6 0.8 maximum_multiply_fusion
  32.4 12.6 %copy.60 = f32[8,2,2,3072]{2,0,1,3:T(8,128)} copy(f32[8,2,2,3072]{3,2,0,1:T(2,128)S(1)} %maximum_multiply_fusion) | data formatting | bytes 786432
  44.9 18.1 %reshape.121 = f32[3072,32]{1,0:T(8,128)} reshape(f32[3072,2,8,2]{3,2,1,0:T(8,128)} %bitcast.54) | data formatting | bytes 786432
  63.2 63.6 %reduce-scatter.4.cloned.1.call-done = f32[256,32]{1,0:T(8,128)} async-done(((f32[3072,32]{1,0:T(8,128)}), f32[256,32]{1,0:T(8,128)}) %reduce-scatter.4.cloned.1.call-update) | async-done | bytes 32784
  126.8 2.1 %reshape.122 = f32[256,2,8,2]{3,2,1,0:T(8,128)S(1)} reshape(f32[256,32]{1,0:T(8,128)} %reduce-scatter.4.cloned.1.call-done) | data formatting | bytes 65536
  129.0 3.4 %copy.57 = f32[8,2,2,256]{0,2,1,3:T(2,128)S(1)} copy(f32[8,2,2,256]{2,0,1,3:T(8,128)S(1)} %bitcast.55) | data formatting | bytes 65536 | tf_op jit(solution)/shard_map/reduce_scatter | solution.py:140
  132.4 1.4 reshape.126
  133.8 6.7 %all-to-all-start = ((f32[2,1,4096]{2,1,0:T(1,128)}), f32[2,1,4096]{2,1,0:T(1,128)S(1)}, u32[]{:S(2)}, u32[]{:S(2)}) async-start(f32[2,1,4096]{2,1,0:T(1,128)} %reshape.126), calls=%async_computation | async-start | bytes 65536 | tf_op jit(solution)/shard_map/all_to_all | solution.py:141
  140.5 0.1 mul.438
  140.6 7.8 %all-to-all-done = f32[2,1,4096]{2,1,0:T(1,128)S(1)} async-done(((f32[2,1,4096]{2,1,0:T(1,128)}), f32[2,1,4096]{2,1,0:T(1,128)S(1)}, u32[]{:S(2)}, u32[]{:S(2)}) %all-to-all-start) | async-done | bytes 32800 | tf_op jit(solution)/shard_map/all_to_all | solution.py:141
  148.3 0.5 broadcast.120
  148.9 0.7 reduce.8
  149.6 0.8 reshape.127
  150.4 0.3 copy.59
  150.7 0.1 subtract_reduce_fusion
  150.9 0.1 stack.39
  150.9 0.1 stack.40
  151.0 0.1 stack.41
  151.1 0.1 stack.42
  151.2 1.9 collective-permute-start.2
  153.1 1.3 collective-permute-start.3
  154.4 8.1 %collective-permute-done.3 = f32[4,2,1,64]{3,2,1,0:T(1,128)S(1)} collective-permute-done((f32[4,2,1,64]{3,2,1,0:T(1,128)S(1)}, f32[4,2,1,64]{3,2,1,0:T(1,128)S(1)}, u32[]{:S(2)}, u32[]{:S(2)}) %collective-permute-start.3) | collective-permute-done | bytes 2080 | tf_op jit(solution)/shard_map/ppermute | solution.py:21
  162.6 1.9 collective-permute-start.4
  164.5 2.4 %collective-permute-start.5 = (f32[4,1,4,64]{3,2,1,0:T(4,128)S(1)}, f32[4,1,4,64]{3,2,1,0:T(4,128)S(1)}, u32[]{:S(2)}, u32[]{:S(2)}) collective-permute-start(f32[4,1,4,64]{3,2,1,0:T(4,128)S(1)} %get-tuple-element.27), channel_id=1, source_target_pairs={{0,1},{1,2},{2,3},{3,4},{4,5},{5,6},{6,7},{7,8},{8,9},{9,10},{10,1... | collective-permute-start | bytes 12296 | tf_op jit(solution)/shard_map/ppermute | solution.py:20
  166.9 0.2 slice_reduce_fusion.2
  167.1 5.1 %collective-permute-done.5 = f32[4,1,4,64]{3,2,1,0:T(4,128)S(1)} collective-permute-done((f32[4,1,4,64]{3,2,1,0:T(4,128)S(1)}, f32[4,1,4,64]{3,2,1,0:T(4,128)S(1)}, u32[]{:S(2)}, u32[]{:S(2)}) %collective-permute-start.5) | collective-permute-done | bytes 4128 | tf_op jit(solution)/shard_map/ppermute | solution.py:20
  172.2 0.1 fusion.58
  172.3 8.3 %collective-permute-start.6 = (f32[4,2,1,64]{3,2,1,0:T(1,128)S(1)}, f32[4,2,1,64]{3,2,1,0:T(1,128)S(1)}, u32[]{:S(2)}, u32[]{:S(2)}) collective-permute-start(f32[4,2,1,64]{3,2,1,0:T(1,128)S(1)} %get-tuple-element.29), channel_id=1, source_target_pairs={{0,32},{32,64},{64,96},{96,128},{128,160},{160,192},{192,224},{224... | collective-permute-start | bytes 6152 | tf_op jit(solution)/shard_map/ppermute | solution.py:20
  180.6 1.3 collective-permute-start.7
  181.9 8.1 %collective-permute-done.7 = f32[4,2,1,64]{3,2,1,0:T(1,128)S(1)} collective-permute-done((f32[4,2,1,64]{3,2,1,0:T(1,128)S(1)}, f32[4,2,1,64]{3,2,1,0:T(1,128)S(1)}, u32[]{:S(2)}, u32[]{:S(2)}) %collective-permute-start.7) | collective-permute-done | bytes 2080 | tf_op jit(solution)/shard_map/ppermute | solution.py:21
  190.0 1.9 collective-permute-start.8
  192.0 2.4 %collective-permute-start.9 = (f32[4,1,4,64]{3,2,1,0:T(4,128)S(1)}, f32[4,1,4,64]{3,2,1,0:T(4,128)S(1)}, u32[]{:S(2)}, u32[]{:S(2)}) collective-permute-start(f32[4,1,4,64]{3,2,1,0:T(4,128)S(1)} %get-tuple-element.25), channel_id=1, source_target_pairs={{0,1},{1,2},{2,3},{3,4},{4,5},{5,6},{6,7},{7,8},{8,9},{9,10},{10,1... | collective-permute-start | bytes 12296 | tf_op jit(solution)/shard_map/ppermute | solution.py:20
  194.4 5.2 %collective-permute-done.9 = f32[4,1,4,64]{3,2,1,0:T(4,128)S(1)} collective-permute-done((f32[4,1,4,64]{3,2,1,0:T(4,128)S(1)}, f32[4,1,4,64]{3,2,1,0:T(4,128)S(1)}, u32[]{:S(2)}, u32[]{:S(2)}) %collective-permute-start.9) | collective-permute-done | bytes 4128 | tf_op jit(solution)/shard_map/ppermute | solution.py:20
  199.6 0.1 fusion.48
  199.7 0.7 reshape.120
  (35 shorter events, 0.3 us)
Async XLA Ops:
  6.5 9.6 %copy-start.6 = (f32[3]{0:T(128)S(1)}, f32[3]{0:T(128)}, u32[]{:S(2)}) copy-start(f32[3]{0:T(128)} %param.14) | copy-start | bytes 40
  6.5 120.3 %reduce-scatter.4.cloned.1.call-start = ((), (), s32[]{:S(2)}) async-start(), calls=%async_computation.2 | async-start | bytes 1703936
  8.3 14.3 %collective-permute-start = (f32[2,1,8,2,1,3072]{5,4,2,3,1,0:T(1,128)S(1)}, f32[2,1,8,2,1,3072]{5,4,2,3,1,0:T(1,128)S(1)}, u32[]{:S(2)}, u32[]{:S(2)}) collective-permute-start(f32[2,1,8,2,1,3072]{5,4,2,3,1,0:T(1,128)S(1)} %get-tuple-element.16), channel_id=1, source_target_pairs={{1,0},{2,1},{3,2},{4,3},{5,4},{6,5},{7,6},{8,7},{9,8},{10,9},{11,1... | collective-permute-start | bytes 1179656 | tf_op jit(solution)/shard_map/ppermute | solution.py:21
  13.6 11.8 %collective-permute-start.1 = (f32[2,1,8,2,1,3072]{5,4,2,3,1,0:T(1,128)S(1)}, f32[2,1,8,2,1,3072]{5,4,2,3,1,0:T(1,128)S(1)}, u32[]{:S(2)}, u32[]{:S(2)}) collective-permute-start(f32[2,1,8,2,1,3072]{5,4,2,3,1,0:T(1,128)S(1)} %get-tuple-element.17), channel_id=1, source_target_pairs={{0,1},{1,2},{2,3},{3,4},{4,5},{5,6},{6,7},{7,8},{8,9},{9,10},{10,1... | collective-permute-start | bytes 1179656 | tf_op jit(solution)/shard_map/ppermute | solution.py:20
  44.9 18.2 %copy-start.5 = (s32[2,128]{1,0:T(2,128)S(1)}, s32[2,128]{1,0:T(2,128)}, u32[]{:S(2)}) copy-start(s32[2,128]{1,0:T(2,128)} %param.20) | copy-start | bytes 3076
  44.9 18.2 %copy-start.1 = (f32[2,128]{1,0:T(2,128)S(1)}, f32[2,128]{1,0:T(2,128)}, u32[]{:S(2)}) copy-start(f32[2,128]{1,0:T(2,128)} %param.19) | copy-start | bytes 3076
  44.9 18.2 %copy-start.2 = (f32[2,128]{1,0:T(2,128)S(1)}, f32[2,128]{1,0:T(2,128)}, u32[]{:S(2)}) copy-start(f32[2,128]{1,0:T(2,128)} %param.17) | copy-start | bytes 3076
  128.9 11.6 %copy-start.7 = (s32[16]{0:T(128)S(1)}, s32[16]{0:T(128)}, u32[]{:S(2)}) copy-start(s32[16]{0:T(128)} %param.15) | copy-start | bytes 196
  128.9 21.7 %copy-start.3 = (f32[2,128]{1,0:T(2,128)S(1)}, f32[2,128]{1,0:T(2,128)}, u32[]{:S(2)}) copy-start(f32[2,128]{1,0:T(2,128)} %param.18) | copy-start | bytes 3076
  129.0 21.9 %copy-start.4 = (f32[2,128]{1,0:T(2,128)S(1)}, f32[2,128]{1,0:T(2,128)}, u32[]{:S(2)}) copy-start(f32[2,128]{1,0:T(2,128)} %param.16) | copy-start | bytes 3076
  129.0 38.0 %copy-start = (f32[4,3]{1,0:T(4,128)S(1)}, f32[4,3]{1,0:T(4,128)}, u32[]{:S(2)}) copy-start(f32[4,3]{1,0:T(4,128)} %param.21) | copy-start | bytes 148
  133.8 14.6 %all-to-all-start = ((f32[2,1,4096]{2,1,0:T(1,128)}), f32[2,1,4096]{2,1,0:T(1,128)S(1)}, u32[]{:S(2)}, u32[]{:S(2)}) async-start(f32[2,1,4096]{2,1,0:T(1,128)} %reshape.126), calls=%async_computation | async-start | bytes 65536 | tf_op jit(solution)/shard_map/all_to_all | solution.py:141
  151.2 3.2 %collective-permute-start.2 = (f32[4,2,1,64]{3,2,1,0:T(1,128)S(1)}, f32[4,2,1,64]{3,2,1,0:T(1,128)S(1)}, u32[]{:S(2)}, u32[]{:S(2)}) collective-permute-start(f32[4,2,1,64]{3,2,1,0:T(1,128)S(1)} %get-tuple-element.31), channel_id=1, source_target_pairs={{0,32},{32,64},{64,96},{96,128},{128,160},{160,192},{192,224},{224... | collective-permute-start | bytes 6152 | tf_op jit(solution)/shard_map/ppermute | solution.py:20
  153.1 9.4 %collective-permute-start.3 = (f32[4,2,1,64]{3,2,1,0:T(1,128)S(1)}, f32[4,2,1,64]{3,2,1,0:T(1,128)S(1)}, u32[]{:S(2)}, u32[]{:S(2)}) collective-permute-start(f32[4,2,1,64]{3,2,1,0:T(1,128)S(1)} %get-tuple-element.30), channel_id=1, source_target_pairs={{32,0},{64,32},{96,64},{128,96},{160,128},{192,160},{224,192},{256... | collective-permute-start | bytes 6152 | tf_op jit(solution)/shard_map/ppermute | solution.py:21
  162.6 4.5 %collective-permute-start.4 = (f32[4,1,4,64]{3,2,1,0:T(4,128)S(1)}, f32[4,1,4,64]{3,2,1,0:T(4,128)S(1)}, u32[]{:S(2)}, u32[]{:S(2)}) collective-permute-start(f32[4,1,4,64]{3,2,1,0:T(4,128)S(1)} %get-tuple-element.26), channel_id=1, source_target_pairs={{1,0},{2,1},{3,2},{4,3},{5,4},{6,5},{7,6},{8,7},{9,8},{10,9},{11,1... | collective-permute-start | bytes 12296 | tf_op jit(solution)/shard_map/ppermute | solution.py:21
  164.5 7.7 %collective-permute-start.5 = (f32[4,1,4,64]{3,2,1,0:T(4,128)S(1)}, f32[4,1,4,64]{3,2,1,0:T(4,128)S(1)}, u32[]{:S(2)}, u32[]{:S(2)}) collective-permute-start(f32[4,1,4,64]{3,2,1,0:T(4,128)S(1)} %get-tuple-element.27), channel_id=1, source_target_pairs={{0,1},{1,2},{2,3},{3,4},{4,5},{5,6},{6,7},{7,8},{8,9},{9,10},{10,1... | collective-permute-start | bytes 12296 | tf_op jit(solution)/shard_map/ppermute | solution.py:20
  172.3 9.6 %collective-permute-start.6 = (f32[4,2,1,64]{3,2,1,0:T(1,128)S(1)}, f32[4,2,1,64]{3,2,1,0:T(1,128)S(1)}, u32[]{:S(2)}, u32[]{:S(2)}) collective-permute-start(f32[4,2,1,64]{3,2,1,0:T(1,128)S(1)} %get-tuple-element.29), channel_id=1, source_target_pairs={{0,32},{32,64},{64,96},{96,128},{128,160},{160,192},{192,224},{224... | collective-permute-start | bytes 6152 | tf_op jit(solution)/shard_map/ppermute | solution.py:20
  180.6 9.4 %collective-permute-start.7 = (f32[4,2,1,64]{3,2,1,0:T(1,128)S(1)}, f32[4,2,1,64]{3,2,1,0:T(1,128)S(1)}, u32[]{:S(2)}, u32[]{:S(2)}) collective-permute-start(f32[4,2,1,64]{3,2,1,0:T(1,128)S(1)} %get-tuple-element.28), channel_id=1, source_target_pairs={{32,0},{64,32},{96,64},{128,96},{160,128},{192,160},{224,192},{256... | collective-permute-start | bytes 6152 | tf_op jit(solution)/shard_map/ppermute | solution.py:21
  190.0 4.3 %collective-permute-start.8 = (f32[4,1,4,64]{3,2,1,0:T(4,128)S(1)}, f32[4,1,4,64]{3,2,1,0:T(4,128)S(1)}, u32[]{:S(2)}, u32[]{:S(2)}) collective-permute-start(f32[4,1,4,64]{3,2,1,0:T(4,128)S(1)} %get-tuple-element.24), channel_id=1, source_target_pairs={{1,0},{2,1},{3,2},{4,3},{5,4},{6,5},{7,6},{8,7},{9,8},{10,9},{11,1... | collective-permute-start | bytes 12296 | tf_op jit(solution)/shard_map/ppermute | solution.py:21
  192.0 7.7 %collective-permute-start.9 = (f32[4,1,4,64]{3,2,1,0:T(4,128)S(1)}, f32[4,1,4,64]{3,2,1,0:T(4,128)S(1)}, u32[]{:S(2)}, u32[]{:S(2)}) collective-permute-start(f32[4,1,4,64]{3,2,1,0:T(4,128)S(1)} %get-tuple-element.25), channel_id=1, source_target_pairs={{0,1},{1,2},{2,3},{3,4},{4,5},{5,6},{6,7},{7,8},{8,9},{9,10},{10,1... | collective-permute-start | bytes 12296 | tf_op jit(solution)/shard_map/ppermute | solution.py:20
Sparse Core Ops, SparseCore 0:
  63.2 63.5 reduce-scatter.3
where the time goes:
time: 208 us; the launch traced here: 207 us
  waiting for transfers between devices  106 us (51%)
  local copies, waits for them, and re-layouts  41.9 us (20%)
  starting transfers between devices  35.3 us (17%)
  between operations  14.4 us (7%)
  other arithmetic  9.26 us (4%)
    unnamed x2, waiting for transfers between devices  63.6 us
    unnamed x21, local copies, waits for them, and re-layouts  35.1 us
    ppermute x5, waiting for transfers between devices, padded_2(): after = lax.ppermute(initial, axis, down)  22.1 us
    ppermute x5, starting transfers between devices, padded_2(): before = lax.ppermute(last, axis, up)  16.9 us
    ppermute x5, waiting for transfers between devices, padded_2(): before = lax.ppermute(last, axis, up)  13 us
    ppermute x5, starting transfers between devices, padded_2(): after = lax.ppermute(initial, axis, down)  11.6 us
    all_to_all x1, waiting for transfers between devices, local(): lax.all_to_all(summed, 'freq', split_axis=3, concat_axis=0, tiled=True)  7.76 us
    all_to_all x1, starting transfers between devices, local(): lax.all_to_all(summed, 'freq', split_axis=3, concat_axis=0, tiled=True)  6.72 us
  transfers between devices with their start and end apart: 12, of which 8 were waited for; matrix products, arithmetic and copies ran while one was open for 0% of the time, Pallas kernels for 0%

commit v1 on v0

v1 whole, which is shorter than its diff:
```python
import functools
import math

import jax
import jax.numpy as jnp
from jax import lax
from jax.experimental import pallas as pl
from jax.experimental.pallas import tpu as pltpu
from jax.sharding import PartitionSpec as P

MESH = pl.DeviceIdType.MESH
GROUPS = 3
NY = 64
LANES = 128


def kernel(
    sizes,
    forward,
    adjoint,
    log_sigma,
    charge,
    log_tau,
    exponent,
    active,
    source_group,
    group_weight,
    frequency_index,
    prior_weight,
    out,
    own,
    rows,
    from_prev,
    from_next,
    params,
    partial,
    arrived,
    centre,
    around,
    derivs,
    yz_corr,
    yz_grad,
    load_sem,
    halo_send,
    halo_recv,
    gather_sem,
    scatter_sem,
    near_send,
    near_recv,
):
    n_src, n_freq, n_space, count = sizes
    chunks = n_src * n_freq
    half = 2 * chunks
    others = chunks - 1
    s, h, b = lax.axis_index("src"), lax.axis_index("freq"), lax.axis_index("space")
    k = s * n_freq + h
    f32 = jnp.float32

    def device(block, chunk):
        return (chunk // n_freq, lax.rem(chunk, n_freq), block)

    loads = [
        pltpu.make_async_copy(field, own.at[i], load_sem.at[i])
        for i, field in enumerate((forward, adjoint))
    ]
    for load in loads:
        load.start()

    has_prev, has_next = b > 0, b < n_space - 1
    has_low, has_high = k > 0, k < chunks - 1
    near = []
    for db in (-1, 0, 1):
        for dk in (-1, 0, 1):
            if db == 0 and dk == 0:
                continue
            there = True
            if db != 0:
                there = has_prev if db < 0 else has_next
            if dk != 0:
                ok = has_low if dk < 0 else has_high
                there = ok if there is True else jnp.logical_and(there, ok)
            near.append((db, dk, there))

    barrier = pltpu.get_barrier_semaphore()

    def greet(i, carry):
        pl.semaphore_signal(
            barrier, inc=1, device_id=device(b, lax.rem(k + 1 + i, chunks)), device_id_type=MESH
        )
        return carry

    lax.fori_loop(0, others, greet, 0)
    expected = jnp.int32(others)
    for db, dk, there in near:
        if db == 0:
            continue

        @pl.when(there)
        def _():
            pl.semaphore_signal(barrier, inc=1, device_id=device(b + db, k + dk), device_id_type=MESH)

        expected = expected + there.astype(jnp.int32)

    mine = pl.ds(pl.multiple_of(8 * k, 8), 8)
    params[mine, :] = jnp.concatenate(
        [log_sigma[...], charge[...], log_tau[...], exponent[...]], axis=0
    )

    for load in loads:
        load.wait()

    def split_rows(f, carry):
        for i in range(2):
            for r in range(2):
                rows[r, f, pl.ds(half * i, half), :] = own[i, f, pl.ds(r, half, stride=2), :]
        return carry

    lax.fori_loop(0, count, split_rows, 0)

    @pl.when(jnp.logical_not(has_prev))
    def _():
        from_prev[...] = jnp.zeros_like(from_prev)

    @pl.when(jnp.logical_not(has_next))
    def _():
        from_next[...] = jnp.zeros_like(from_next)

    for db, dk, there in near:
        slot = (db + 1) * 3 + dk + 1

        @pl.when(jnp.logical_not(there))
        def _():
            around[slot] = jnp.zeros((8, LANES), f32)

    pl.semaphore_wait(barrier, expected)

    def up(f):
        return pltpu.make_async_remote_copy(
            src_ref=rows.at[1, f],
            dst_ref=from_prev.at[f],
            send_sem=halo_send.at[0, f],
            recv_sem=halo_recv.at[0, f],
            device_id=device(b + 1, k),
            device_id_type=MESH,
        )

    def down(f):
        return pltpu.make_async_remote_copy(
            src_ref=rows.at[0, f],
            dst_ref=from_next.at[f],
            send_sem=halo_send.at[1, f],
            recv_sem=halo_recv.at[1, f],
            device_id=device(b - 1, k),
            device_id_type=MESH,
        )

    def send_halo(f, carry):
        @pl.when(has_next)
        def _():
            up(f).start()

        @pl.when(has_prev)
        def _():
            down(f).start()

        return carry

    lax.fori_loop(0, count, send_halo, 0)

    def send_params(i, carry):
        pltpu.make_async_remote_copy(
            src_ref=params.at[mine],
            dst_ref=params.at[mine],
            send_sem=gather_sem.at[0],
            recv_sem=gather_sem.at[1],
            device_id=device(b, lax.rem(k + 1 + i, chunks)),
            device_id_type=MESH,
        ).start()
        return carry

    lax.fori_loop(0, others, send_params, 0)

    lane = lax.broadcasted_iota(jnp.int32, (chunks, LANES), 1)
    line = lax.broadcasted_iota(jnp.int32, (chunks, LANES), 0)
    low = lane < NY
    y_pos = jnp.bitwise_and(lane, NY - 1)
    y_last, y_first = y_pos == NY - 1, y_pos == 0
    z_last, z_first = line == chunks - 1, line == 0

    def differences(u):
        grad_y = jnp.where(y_last, 0.0, pltpu.roll(u, LANES - 1, 1)) - jnp.where(
            y_first, 0.0, pltpu.roll(u, 1, 1)
        )
        turned = pltpu.roll(u, NY, 1)
        above = jnp.where(z_last, 0.0, pltpu.roll(turned, chunks - 1, 0))
        below = jnp.where(z_first, 0.0, pltpu.roll(turned, 1, 0))
        return grad_y, jnp.where(low, turned - below, above - turned)

    def correlate_yz(f, carry):
        for r in range(2):
            grads = [
                differences(rows[r, f, pl.ds(chunks * i, chunks), :]) for i in range(4)
            ]
            (fr_y, fr_z), (fi_y, fi_z), (ar_y, ar_z), (ai_y, ai_z) = grads
            yz_corr[f, r, 0] = fr_y * ar_y - fi_y * ai_y + (fr_z * ar_z - fi_z * ai_z)
            yz_corr[f, r, 1] = fr_y * ai_y + fi_y * ar_y + (fr_z * ai_z + fi_z * ar_z)
        return carry

    lax.fori_loop(0, count, correlate_yz, 0)

    all_tiles = pl.ds(0, 8 * others)
    gathered = pltpu.make_async_remote_copy(
        src_ref=arrived.at[all_tiles],
        dst_ref=params.at[all_tiles],
        send_sem=gather_sem.at[0],
        recv_sem=gather_sem.at[1],
        device_id=device(b, lax.rem(k + 1, chunks)),
        device_id_type=MESH,
    )
    gathered.wait_recv()

    weight = jnp.float32(0.0)
    for g in range(GROUPS):
        weight = weight + jnp.where(source_group[0] == g, group_weight[g], 0.0)
    scale = weight * (0.25 / math.sqrt(n_src * n_freq * count))

    for r in range(2):
        sigma, chg, tau, expo = (
            params[pl.ds(2 * p + r, chunks, stride=8), :] for p in range(4)
        )
        sigma = jnp.exp(sigma) * scale
        angle = expo * (0.5 * math.pi)
        cosine, sine = jnp.cos(angle), jnp.sin(angle)
        rest = 1.0 - chg
        q_scale = sigma * chg

        def chain(f, totals):
            index = frequency_index[h * count + f].astype(f32)
            log_omega = math.log(2.0 * math.pi) + math.log(10.0) * (
                -1.0 + (4.0 / (n_freq * count - 1)) * index
            )
            log_product = log_omega + tau
            amplitude = jnp.exp(expo * log_product)
            z_r, z_i = amplitude * cosine, amplitude * sine
            d_r, d_i = 1.0 + rest * z_r, rest * z_i
            inverse = 1.0 / (d_r * d_r + d_i * d_i)
            r_r, r_i = d_r * inverse, -d_i * inverse
            s_r, s_i = (1.0 + z_r) * r_r - z_i * r_i, (1.0 + z_r) * r_i + z_i * r_r
            t_r, t_i = z_r * r_r - z_i * r_i, z_r * r_i + z_i * r_r
            s_r, s_i = sigma * s_r, sigma * s_i
            q_r, q_i = q_scale * (t_r * r_r - t_i * r_i), q_scale * (t_r * r_i + t_i * r_r)
            parts = (
                (s_r, s_i),
                (s_r * t_r - s_i * t_i, s_r * t_i + s_i * t_r),
                (expo * q_r, expo * q_i),
                (
                    q_r * log_product - (0.5 * math.pi) * q_i,
                    (0.5 * math.pi) * q_r + q_i * log_product,
                ),
            )
            c_r, c_i = yz_corr[f, r, 0], yz_corr[f, r, 1]
            new = []
            for p, (part_r, part_i) in enumerate(parts):
                derivs[f, r, 2 * p] = part_r
                derivs[f, r, 2 * p + 1] = part_i
                new.append(totals[p] + (part_r * c_r - part_i * c_i))
            return tuple(new)

        zeros = jnp.zeros((chunks, LANES), f32)
        totals = lax.fori_loop(0, count, chain, (zeros,) * 4)
        for p in range(4):
            yz_grad[r, p] = totals[p]

    def add_x(f, totals):
        @pl.when(has_prev)
        def _():
            up(f).wait_recv()

        @pl.when(has_next)
        def _():
            down(f).wait_recv()

        new = []
        for r in range(2):
            ahead = rows.at[1, f] if r == 0 else from_next.at[f]
            behind = from_prev.at[f] if r == 0 else rows.at[0, f]
            f_r, f_i, a_r, a_i = (
                ahead[pl.ds(chunks * i, chunks), :] - behind[pl.ds(chunks * i, chunks), :]
                for i in range(4)
            )
            c_r, c_i = f_r * a_r - f_i * a_i, f_r * a_i + f_i * a_r
            for p in range(4):
                new.append(
                    totals[4 * r + p] + (derivs[f, r, 2 * p] * c_r - derivs[f, r, 2 * p + 1] * c_i)
                )
        return tuple(new)

    totals = lax.fori_loop(
        0, count, add_x, tuple(yz_grad[r, p] for r in range(2) for p in range(4))
    )
    for r in range(2):
        for p in range(4):
            partial[pl.ds(2 * p + r, chunks, stride=8), :] = totals[4 * r + p]

    def send_partial(i, carry):
        target = lax.rem(k + 1 + i, chunks)
        pltpu.make_async_remote_copy(
            src_ref=partial.at[pl.ds(pl.multiple_of(8 * target, 8), 8)],
            dst_ref=arrived.at[pl.ds(pl.multiple_of(8 * i, 8), 8)],
            send_sem=scatter_sem.at[0],
            recv_sem=scatter_sem.at[1],
            device_id=device(b, target),
            device_id_type=MESH,
        ).start()
        return carry

    lax.fori_loop(0, others, send_partial, 0)
    mask = jnp.concatenate([active[...].astype(f32)] * 4, axis=0)
    scattered = pltpu.make_async_remote_copy(
        src_ref=partial.at[all_tiles],
        dst_ref=arrived.at[all_tiles],
        send_sem=scatter_sem.at[0],
        recv_sem=scatter_sem.at[1],
        device_id=device(b, lax.rem(k + 1, chunks)),
        device_id_type=MESH,
    )
    scattered.wait_recv()
    tiles = [partial[mine, :]] + [arrived[pl.ds(8 * i, 8), :] for i in range(others)]
    while len(tiles) > 1:
        tiles = [
            tiles[i] + tiles[i + 1] if i + 1 < len(tiles) else tiles[i]
            for i in range(0, len(tiles), 2)
        ]
    masked = tiles[0] * mask
    centre[...] = masked

    def to_near(db, dk):
        slot = (1 - db) * 3 + 1 - dk
        return pltpu.make_async_remote_copy(
            src_ref=centre,
            dst_ref=around.at[slot],
            send_sem=near_send.at[slot],
            recv_sem=near_recv.at[slot],
            device_id=device(b + db, k + dk),
            device_id_type=MESH,
        )

    for db, dk, there in near:

        @pl.when(there)
        def _():
            to_near(db, dk).start()

    tile_lane = lax.broadcasted_iota(jnp.int32, (8, LANES), 1)
    tile_line = lax.broadcasted_iota(jnp.int32, (8, LANES), 0)
    tile_low = tile_lane < NY
    tile_y = jnp.bitwise_and(tile_lane, NY - 1)
    top, bottom = tile_y == NY - 1, tile_y == 0
    first_row = jnp.bitwise_and(tile_line, 1) == 0
    smooth = []
    for d in range(3):
        w = jnp.full((8, LANES), prior_weight[0, d], f32)
        for p in range(1, 4):
            w = jnp.where(tile_line >= 2 * p, prior_weight[p, d], w)
        smooth.append(w)

    def one_pass(mid, prev, after, lower, upper):
        x_sum = jnp.where(first_row, pltpu.roll(mid, 7, 0), pltpu.roll(after, 1, 0)) + jnp.where(
            first_row, pltpu.roll(prev, 7, 0), pltpu.roll(mid, 1, 0)
        )
        y_sum = jnp.where(top, 0.0, pltpu.roll(mid, LANES - 1, 1)) + jnp.where(
            bottom, 0.0, pltpu.roll(mid, 1, 1)
        )
        turned = pltpu.roll(mid, NY, 1)
        z_sum = jnp.where(tile_low, turned, pltpu.roll(upper, NY, 1)) + jnp.where(
            tile_low, pltpu.roll(lower, NY, 1), turned
        )
        twice = 2.0 * mid
        return (
            mid
            + smooth[0] * (x_sum - twice)
            + smooth[1] * (y_sum - twice)
            + smooth[2] * (z_sum - twice)
        )

    for db, dk, there in near:

        @pl.when(there)
        def _():
            to_near(-db, -dk).wait_recv()

    def tile(db, dk):
        return masked if db == 0 and dk == 0 else around[(db + 1) * 3 + dk + 1]

    empty = jnp.zeros((8, LANES), f32)

    def inside(there, value):
        return jnp.where(there, value, 0.0)

    mid = one_pass(masked, tile(-1, 0), tile(1, 0), tile(0, -1), tile(0, 1))
    prev = one_pass(tile(-1, 0), empty, masked, tile(-1, -1), tile(-1, 1))
    after = one_pass(tile(1, 0), masked, empty, tile(1, -1), tile(1, 1))
    lower = one_pass(tile(0, -1), tile(-1, -1), tile(1, -1), empty, masked)
    upper = one_pass(tile(0, 1), tile(-1, 1), tile(1, 1), masked, empty)
    out[...] = one_pass(
        mid,
        inside(has_prev, prev),
        inside(has_next, after),
        inside(has_low, lower),
        inside(has_high, upper),
    )

    def sent_halo(f, carry):
        @pl.when(has_next)
        def _():
            up(f).wait_send()

        @pl.when(has_prev)
        def _():
            down(f).wait_send()

        return carry

    lax.fori_loop(0, count, sent_halo, 0)
    gathered.wait_send()
    scattered.wait_send()
    for db, dk, there in near:

        @pl.when(there)
        def _():
            to_near(db, dk).wait_send()


def solution(mesh):
    n_src, n_freq, n_space = mesh.shape["src"], mesh.shape["freq"], mesh.shape["space"]
    chunks = n_src * n_freq

    def local(
        forward,
        adjoint,
        source_group,
        group_weight,
        frequency_index,
        log_sigma,
        charge,
        log_tau,
        exponent,
        active,
        prior_weight,
    ):
        count = forward.shape[1]

        def lines(field):
            split = field.reshape(count, 2, 2, chunks, LANES)
            return split.transpose(0, 1, 3, 2, 4).reshape(count, 4 * chunks, LANES)

        any_spec = pl.BlockSpec(memory_space=pl.ANY)
        vmem = pl.BlockSpec(memory_space=pltpu.VMEM)
        smem = pl.BlockSpec(memory_space=pltpu.SMEM)
        f32 = jnp.float32
        result = pl.pallas_call(
            functools.partial(kernel, (n_src, n_freq, n_space, count)),
            out_shape=jax.ShapeDtypeStruct((8, LANES), f32),
            in_specs=[any_spec] * 2 + [vmem] * 5 + [smem] * 4,
            out_specs=vmem,
            scratch_shapes=[
                pltpu.VMEM((2, count, 4 * chunks, LANES), f32),
                pltpu.VMEM((2, count, 4 * chunks, LANES), f32),
                pltpu.VMEM((count, 4 * chunks, LANES), f32),
                pltpu.VMEM((count, 4 * chunks, LANES), f32),
                pltpu.VMEM((8 * chunks, LANES), f32),
                pltpu.VMEM((8 * chunks, LANES), f32),
                pltpu.VMEM((8 * chunks, LANES), f32),
                pltpu.VMEM((8, LANES), f32),
                pltpu.VMEM((9, 8, LANES), f32),
                pltpu.VMEM((count, 2, 8, chunks, LANES), f32),
                pltpu.VMEM((count, 2, 2, chunks, LANES), f32),
                pltpu.VMEM((2, 4, chunks, LANES), f32),
                pltpu.SemaphoreType.DMA((2,)),
                pltpu.SemaphoreType.DMA((2, count)),
                pltpu.SemaphoreType.DMA((2, count)),
                pltpu.SemaphoreType.DMA((2,)),
                pltpu.SemaphoreType.DMA((2,)),
                pltpu.SemaphoreType.DMA((9,)),
                pltpu.SemaphoreType.DMA((9,)),
            ],
            compiler_params=pltpu.CompilerParams(
                collective_id=0, has_side_effects=True, vmem_limit_bytes=32 * 1024 * 1024
            ),
        )(
            lines(forward),
            lines(adjoint),
            log_sigma,
            charge,
            log_tau,
            exponent,
            active,
            source_group,
            group_weight,
            frequency_index,
            prior_weight,
        )
        return result.reshape(4, 2, LANES)

    placed = (
        P("src", "freq", None, "space", None),
        P("src", "freq", None, "space", None),
        P("src"),
        P(),
        P(),
        P("space", ("src", "freq")),
        P("space", ("src", "freq")),
        P("space", ("src", "freq")),
        P("space", ("src", "freq")),
        P("space", ("src", "freq")),
        P(),
    )
    return jax.shard_map(
        local,
        mesh=mesh,
        in_specs=placed,
        out_specs=P(None, "space", ("src", "freq")),
        check_vma=False,
    )
```

time: 208 us -> 56.5 us (0.27)
  the two profiles are of different devices: /device:TPU:6 before, /device:TPU:1 now
where the time goes in v1:
time: 56.5 us; the launch traced here: 56.2 us
  Pallas kernels  50.2 us (89%)
  local copies, waits for them, and re-layouts  5.26 us (9%)
  between operations  0.74 us (1%)
    pallas_call x1, Pallas kernels, local(): pl.pallas_call(functools.partial(kernel, (n_src, n_freq, n_space, count))...  50.2 us
    unnamed x21, local copies, waits for them, and re-layouts  5.26 us

profile of v1, /device:TPU:1, one launch (start us, length us, event | category | flops | bytes accessed | tf_op | source)
XLA Modules:
  0.0 56.2 jit_solution(1472979508336996770)
XLA Ops:
  0.0 0.0 copy-start.4
  0.0 0.0 copy-start.5
  0.7 0.0 copy-start.2
  0.7 0.0 copy-start.3
  0.7 0.0 copy-start.8
  0.7 0.0 copy-done.4
  0.7 0.0 copy-done.5
  0.7 0.6 %copy-done.2 = f32[4,3]{1,0:T(4,128)S(1)} copy-done((f32[4,3]{1,0:T(4,128)S(1)}, f32[4,3]{1,0:T(4,128)}, u32[]{:S(2)}) %copy-start.2) | copy-done | bytes 72
  1.4 0.0 copy-done.3
  1.4 0.0 copy-done.8
  1.4 0.0 copy-start
  1.4 1.0 %copy-done = f32[1,8,2,2,3072]{4,3,2,1,0:T(2,128)S(1)} copy-done((f32[1,8,2,2,3072]{4,3,2,1,0:T(2,128)S(1)}, f32[1,8,2,2,3072]{4,3,2,1,0:T(2,128)}, u32[]{:S(2)}) %copy-start) | copy-done | bytes 393240
  2.4 0.0 copy-start.1
  2.4 1.0 %copy-done.1 = f32[1,8,2,2,3072]{4,3,2,1,0:T(2,128)S(1)} copy-done((f32[1,8,2,2,3072]{4,3,2,1,0:T(2,128)S(1)}, f32[1,8,2,2,3072]{4,3,2,1,0:T(2,128)}, u32[]{:S(2)}) %copy-start.1) | copy-done | bytes 393240
  3.4 0.0 copy-start.6
  3.4 0.7 %copy-done.6 = f32[2,128]{1,0:T(2,128)S(1)} copy-done((f32[2,128]{1,0:T(2,128)S(1)}, f32[2,128]{1,0:T(2,128)}, u32[]{:S(2)}) %copy-start.6) | copy-done | bytes 1048
  4.1 0.0 copy-start.7
  4.1 0.7 %copy-done.7 = s32[2,128]{1,0:T(2,128)S(1)} copy-done((s32[2,128]{1,0:T(2,128)S(1)}, s32[2,128]{1,0:T(2,128)}, u32[]{:S(2)}) %copy-start.7) | copy-done | bytes 1048
  4.7 0.0 copy-start.9
  4.7 0.7 %copy-done.9 = s32[16]{0:T(128)S(1)} copy-done((s32[16]{0:T(128)S(1)}, s32[16]{0:T(128)}, u32[]{:S(2)}) %copy-start.9) | copy-done | bytes 88
  5.4 50.2 %shard_map.109 = f32[8,128]{1,0:T(8,128)S(1)} custom-call(f32[8,96,128]{2,1,0:T(8,128)S(1)} %bitcast.11, f32[8,96,128]{2,1,0:T(8,128)S(1)} %bitcast.12, f32[2,128]{1,0:T(2,128)S(1)} %copy-done.3, f32[2,128]{1,0:T(2,128)S(1)} %copy-done.4, f32[2,128]{1,0:T(2,128)S(1)} %copy-done.5, f32[2,128]{1,0:T(2,128)S(1)} %copy-done.6, s32[2,128]{1,0:T(2,128)S(1)} %copy-done.7, ...), custom_call_target="tpu_custom_call" | custom-call | tf_op jit(solution)/shard_map/pallas_call | solution.py:461
  55.6 0.6 %copy.16 = f32[4,2,128]{2,1,0:T(2,128)} copy(f32[4,2,128]{2,1,0:T(2,128)S(1)} %bitcast.13) | data formatting | bytes 8192
Async XLA Ops:
  0.0 0.7 %copy-start.4 = (f32[2,128]{1,0:T(2,128)S(1)}, f32[2,128]{1,0:T(2,128)}, u32[]{:S(2)}) copy-start(f32[2,128]{1,0:T(2,128)} %charge.1) | copy-start | bytes 3076
  0.0 0.7 %copy-start.5 = (f32[2,128]{1,0:T(2,128)S(1)}, f32[2,128]{1,0:T(2,128)}, u32[]{:S(2)}) copy-start(f32[2,128]{1,0:T(2,128)} %log_tau.1) | copy-start | bytes 3076
  0.7 0.7 %copy-start.2 = (f32[4,3]{1,0:T(4,128)S(1)}, f32[4,3]{1,0:T(4,128)}, u32[]{:S(2)}) copy-start(f32[4,3]{1,0:T(4,128)} %prior_weight.1) | copy-start | bytes 148
  0.7 0.7 %copy-start.3 = (f32[2,128]{1,0:T(2,128)S(1)}, f32[2,128]{1,0:T(2,128)}, u32[]{:S(2)}) copy-start(f32[2,128]{1,0:T(2,128)} %log_sigma.1) | copy-start | bytes 3076
  0.7 0.7 %copy-start.8 = (f32[3]{0:T(128)S(1)}, f32[3]{0:T(128)}, u32[]{:S(2)}) copy-start(f32[3]{0:T(128)} %group_weight.1) | copy-start | bytes 40
  1.4 1.0 %copy-start = (f32[1,8,2,2,3072]{4,3,2,1,0:T(2,128)S(1)}, f32[1,8,2,2,3072]{4,3,2,1,0:T(2,128)}, u32[]{:S(2)}) copy-start(f32[1,8,2,2,3072]{4,3,2,1,0:T(2,128)} %param.11) | copy-start | bytes 1179652
  2.4 1.0 %copy-start.1 = (f32[1,8,2,2,3072]{4,3,2,1,0:T(2,128)S(1)}, f32[1,8,2,2,3072]{4,3,2,1,0:T(2,128)}, u32[]{:S(2)}) copy-start(f32[1,8,2,2,3072]{4,3,2,1,0:T(2,128)} %param.12) | copy-start | bytes 1179652
  3.4 0.7 %copy-start.6 = (f32[2,128]{1,0:T(2,128)S(1)}, f32[2,128]{1,0:T(2,128)}, u32[]{:S(2)}) copy-start(f32[2,128]{1,0:T(2,128)} %exponent.1) | copy-start | bytes 3076
  4.1 0.7 %copy-start.7 = (s32[2,128]{1,0:T(2,128)S(1)}, s32[2,128]{1,0:T(2,128)}, u32[]{:S(2)}) copy-start(s32[2,128]{1,0:T(2,128)} %active.1) | copy-start | bytes 3076
  4.7 0.7 %copy-start.9 = (s32[16]{0:T(128)S(1)}, s32[16]{0:T(128)}, u32[]{:S(2)}) copy-start(s32[16]{0:T(128)} %frequency_index.1) | copy-start | bytes 196

commit v2 on v1

--- a/solution.py
+++ b/solution.py
@@ -22,89 +22,128 @@
     charge,
     log_tau,
     exponent,
-    active,
+    active_in,
     source_group,
     group_weight,
     frequency_index,
     prior_weight,
     out,
+    cell_params,
+    active,
     own,
     rows,
     from_prev,
     from_next,
     params,
+    masks,
     partial,
     arrived,
-    centre,
-    around,
+    window,
     derivs,
     yz_corr,
     yz_grad,
     load_sem,
+    small_sem,
     halo_send,
     halo_recv,
+    pair_send,
+    pair_recv,
     gather_sem,
     scatter_sem,
     near_send,
     near_recv,
 ):
-    n_src, n_freq, n_space, count = sizes
-    chunks = n_src * n_freq
+    n_src, n_space, count = sizes
+    chunks = 2 * n_src
     half = 2 * chunks
-    others = chunks - 1
     s, h, b = lax.axis_index("src"), lax.axis_index("freq"), lax.axis_index("space")
-    k = s * n_freq + h
+    k = 2 * s + h
     f32 = jnp.float32
-
-    def device(block, chunk):
-        return (chunk // n_freq, lax.rem(chunk, n_freq), block)
+    steps = sorted(range(1, n_src), key=lambda step: -min(step, n_src - step))
+
+    def along(step):
+        return lax.rem(s + step, n_src)
 
     loads = [
         pltpu.make_async_copy(field, own.at[i], load_sem.at[i])
         for i, field in enumerate((forward, adjoint))
     ]
-    for load in loads:
+    small = [
+        pltpu.make_async_copy(source, target, small_sem.at[i])
+        for i, (source, target) in enumerate(
+            (
+                (log_sigma, cell_params.at[0]),
+                (charge, cell_params.at[1]),
+                (log_tau, cell_params.at[2]),
+                (exponent, cell_params.at[3]),
+                (active_in, active),
+            )
+        )
+    ]
+    for load in loads + small:
         load.start()
 
     has_prev, has_next = b > 0, b < n_space - 1
-    has_low, has_high = k > 0, k < chunks - 1
-    near = []
+    beside = {-1: has_prev, 0: None, 1: has_next}
+
+    def both(first, second):
+        if first is None or second is None:
+            return second if first is None else first
+        return jnp.logical_and(first, second)
+
+    def in_window(slot, share, start, size):
+        return pl.ds(pl.multiple_of(48 * slot + 24 * share + start, 8), size)
+
+    def where_there(there, act):
+        if there is None:
+            act()
+        else:
+            pl.when(there)(act)
+
+    side, away = s - 1 + 2 * h, s + 1 - 2 * h
+    has_side = jnp.logical_and(side >= 0, side < n_src)
+    has_away = jnp.logical_and(away >= 0, away < n_src)
+    sends = []
     for db in (-1, 0, 1):
-        for dk in (-1, 0, 1):
-            if db == 0 and dk == 0:
-                continue
-            there = True
-            if db != 0:
-                there = has_prev if db < 0 else has_next
-            if dk != 0:
-                ok = has_low if dk < 0 else has_high
-                there = ok if there is True else jnp.logical_and(there, ok)
-            near.append((db, dk, there))
+        if db != 0:
+            sends.append((beside[db], 0, (s, h, b + db), (8 - 8 * h, 16), 1 - db, 0))
+        sends.append((beside[db], 0, (s, 1 - h, b + db), (8 * h, 16), 1 - db, 0))
+        there = both(has_away, beside[db])
+        sends.append((there, 8 - 8 * h, (away, h, b + db), (16 * h, 8), 1 - db, 1))
+        there = both(has_side, beside[db])
+        sends.append((there, 8 * h, (side, 1 - h, b + db), (16 - 16 * h, 8), 1 - db, 1))
+    receives = []
+    for db in (-1, 0, 1):
+        if db != 0:
+            receives.append((beside[db], (s, h, b + db), (8 - 8 * h, 16), 1 + db, h, 0))
+        receives.append((beside[db], (s, 1 - h, b + db), (8 - 8 * h, 16), 1 + db, 1 - h, 0))
+        for other in (h, 1 - h):
+            there = both(has_side, beside[db])
+            receives.append((there, (side, other, b + db), (16 * h, 8), 1 + db, other, 1))
 
     barrier = pltpu.get_barrier_semaphore()
 
-    def greet(i, carry):
-        pl.semaphore_signal(
-            barrier, inc=1, device_id=device(b, lax.rem(k + 1 + i, chunks)), device_id_type=MESH
-        )
-        return carry
-
-    lax.fori_loop(0, others, greet, 0)
-    expected = jnp.int32(others)
-    for db, dk, there in near:
-        if db == 0:
+    def greet(device):
+        pl.semaphore_signal(barrier, inc=1, device_id=device, device_id_type=MESH)
+
+    for there, device, _, slot, other, kind in receives:
+        if kind == 1 and slot == 1 and other is h:
             continue
-
-        @pl.when(there)
-        def _():
-            pl.semaphore_signal(barrier, inc=1, device_id=device(b + db, k + dk), device_id_type=MESH)
-
-        expected = expected + there.astype(jnp.int32)
+        where_there(there, functools.partial(greet, device))
+    for step in steps:
+        greet((along(step), h, b))
+    one = jnp.int32(1)
+    sides = has_prev.astype(jnp.int32) + has_next.astype(jnp.int32)
+    expected = n_src - 1 + one + 2 * sides
+    expected = expected + has_side.astype(jnp.int32) * (1 + sides)
+    expected = expected + has_away.astype(jnp.int32) * sides
 
     mine = pl.ds(pl.multiple_of(8 * k, 8), 8)
-    params[mine, :] = jnp.concatenate(
-        [log_sigma[...], charge[...], log_tau[...], exponent[...]], axis=0
-    )
+    my_half = pl.ds(pl.multiple_of(8 * h, 8), 8)
+    for load in small:
+        load.wait()
+    params[mine, :] = jnp.concatenate([cell_params[p] for p in range(4)], axis=0)
+    masks[my_half, :] = jnp.concatenate([active[...].astype(f32)] * 4, axis=0)
 
     for load in loads:
         load.wait()
@@ -120,19 +159,33 @@
     @pl.when(jnp.logical_not(has_prev))
     def _():
         from_prev[...] = jnp.zeros_like(from_prev)
+        window[pl.ds(0, 48), :] = jnp.zeros((48, LANES), f32)
 
     @pl.when(jnp.logical_not(has_next))
     def _():
         from_next[...] = jnp.zeros_like(from_next)
-
-    for db, dk, there in near:
-        slot = (db + 1) * 3 + dk + 1
-
-        @pl.when(jnp.logical_not(there))
-        def _():
-            around[slot] = jnp.zeros((8, LANES), f32)
+        window[pl.ds(96, 48), :] = jnp.zeros((48, LANES), f32)
+
+    @pl.when(jnp.logical_not(has_side))
+    def _():
+        for db in range(3):
+            for other in range(2):
+                window[in_window(db, other, 16 * h, 8), :] = jnp.zeros((8, LANES), f32)
 
     pl.semaphore_wait(barrier, expected)
+
+    def to_partner(i):
+        ref, part = ((params, mine), (masks, my_half))[i]
+        return pltpu.make_async_remote_copy(
+            src_ref=ref.at[part],
+            dst_ref=ref.at[part],
+            send_sem=pair_send.at[i],
+            recv_sem=pair_recv.at[i],
+            device_id=(s, 1 - h, b),
+            device_id_type=MESH,
+        )
+
+    to_partner(0).start()
 
     def up(f):
         return pltpu.make_async_remote_copy(
@@ -140,7 +193,7 @@
             dst_ref=from_prev.at[f],
             send_sem=halo_send.at[0, f],
             recv_sem=halo_recv.at[0, f],
-            device_id=device(b + 1, k),
+            device_id=(s, h, b + 1),
             device_id_type=MESH,
         )
 
@@ -150,7 +203,7 @@
             dst_ref=from_next.at[f],
             send_sem=halo_send.at[1, f],
             recv_sem=halo_recv.at[1, f],
-            device_id=device(b - 1, k),
+            device_id=(s, h, b - 1),
             device_id_type=MESH,
         )
 
@@ -166,19 +219,7 @@
         return carry
 
     lax.fori_loop(0, count, send_halo, 0)
-
-    def send_params(i, carry):
-        pltpu.make_async_remote_copy(
-            src_ref=params.at[mine],
-            dst_ref=params.at[mine],
-            send_sem=gather_sem.at[0],
-            recv_sem=gather_sem.at[1],
-            device_id=device(b, lax.rem(k + 1 + i, chunks)),
-            device_id_type=MESH,
-        ).start()
-        return carry
-
-    lax.fori_loop(0, others, send_params, 0)
+    to_partner(1).start()
 
     lane = lax.broadcasted_iota(jnp.int32, (chunks, LANES), 1)
     line = lax.broadcasted_iota(jnp.int32, (chunks, LANES), 0)
@@ -208,13 +249,24 @@
 
     lax.fori_loop(0, count, correlate_yz, 0)
 
-    all_tiles = pl.ds(0, 8 * others)
+    to_partner(0).wait_recv()
+    pair = pl.ds(pl.multiple_of(16 * s, 16), 16)
+    for step in steps:
+        pltpu.make_async_remote_copy(
+            src_ref=params.at[pair],
+            dst_ref=params.at[pair],
+            send_sem=gather_sem.at[0],
+            recv_sem=gather_sem.at[1],
+            device_id=(along(step), h, b),
+            device_id_type=MESH,
+        ).start()
+    others = pl.ds(0, 16 * (n_src - 1))
     gathered = pltpu.make_async_remote_copy(
-        src_ref=arrived.at[all_tiles],
-        dst_ref=params.at[all_tiles],
+        src_ref=partial.at[others],
+        dst_ref=params.at[others],
         send_sem=gather_sem.at[0],
         recv_sem=gather_sem.at[1],
-        device_id=device(b, lax.rem(k + 1, chunks)),
+        device_id=(along(1), h, b),
         device_id_type=MESH,
     )
     gathered.wait_recv()
@@ -222,7 +274,7 @@
     weight = jnp.float32(0.0)
     for g in range(GROUPS):
         weight = weight + jnp.where(source_group[0] == g, group_weight[g], 0.0)
-    scale = weight * (0.25 / math.sqrt(n_src * n_freq * count))
+    scale = weight * (0.25 / math.sqrt(n_src * 2 * count))
 
     for r in range(2):
         sigma, chg, tau, expo = (
@@ -237,7 +289,7 @@
         def chain(f, totals):
             index = frequency_index[h * count + f].astype(f32)
             log_omega = math.log(2.0 * math.pi) + math.log(10.0) * (
-                -1.0 + (4.0 / (n_freq * count - 1)) * index
+                -1.0 + (4.0 / (2 * count - 1)) * index
             )
             log_product = log_omega + tau
             amplitude = jnp.exp(expo * log_product)
@@ -302,54 +354,60 @@
         for p in range(4):
             partial[pl.ds(2 * p + r, chunks, stride=8), :] = totals[4 * r + p]
 
-    def send_partial(i, carry):
-        target = lax.rem(k + 1 + i, chunks)
+    for i, step in enumerate(steps):
+        to = along(step)
         pltpu.make_async_remote_copy(
-            src_ref=partial.at[pl.ds(pl.multiple_of(8 * target, 8), 8)],
-            dst_ref=arrived.at[pl.ds(pl.multiple_of(8 * i, 8), 8)],
+            src_ref=partial.at[pl.ds(pl.multiple_of(16 * to, 16), 16)],
+            dst_ref=arrived.at[pl.ds(16 * i, 16)],
             send_sem=scatter_sem.at[0],
             recv_sem=scatter_sem.at[1],
-            device_id=device(b, target),
+            device_id=(to, h, b),
             device_id_type=MESH,
         ).start()
-        return carry
-
-    lax.fori_loop(0, others, send_partial, 0)
-    mask = jnp.concatenate([active[...].astype(f32)] * 4, axis=0)
+    to_partner(1).wait_recv()
+    mask = masks[...]
     scattered = pltpu.make_async_remote_copy(
-        src_ref=partial.at[all_tiles],
-        dst_ref=arrived.at[all_tiles],
+        src_ref=partial.at[others],
+        dst_ref=arrived.at[others],
         send_sem=scatter_sem.at[0],
         recv_sem=scatter_sem.at[1],
-        device_id=device(b, lax.rem(k + 1, chunks)),
+        device_id=(along(1), h, b),
         device_id_type=MESH,
     )
     scattered.wait_recv()
-    tiles = [partial[mine, :]] + [arrived[pl.ds(8 * i, 8), :] for i in range(others)]
+    tiles = [partial[pair, :]] + [arrived[pl.ds(16 * i, 16), :] for i in range(n_src - 1)]
     while len(tiles) > 1:
         tiles = [
             tiles[i] + tiles[i + 1] if i + 1 < len(tiles) else tiles[i]
             for i in range(0, len(tiles), 2)
         ]
-    masked = tiles[0] * mask
-    centre[...] = masked
-
-    def to_near(db, dk):
-        slot = (1 - db) * 3 + 1 - dk
+    window[in_window(1, h, 8 - 8 * h, 16), :] = tiles[0] * mask
+
+    def to_near(entry):
+        there, part, device, (start, size), slot, kind = sends[entry]
         return pltpu.make_async_remote_copy(
-            src_ref=centre,
-            dst_ref=around.at[slot],
-            send_sem=near_send.at[slot],
-            recv_sem=near_recv.at[slot],
-            device_id=device(b + db, k + dk),
-            device_id_type=MESH,
-        )
-
-    for db, dk, there in near:
-
-        @pl.when(there)
-        def _():
-            to_near(db, dk).start()
+            src_ref=window.at[in_window(1, h, 8 - 8 * h + part, size)],
+            dst_ref=window.at[in_window(slot, h, start, size)],
+            send_sem=near_send.at[entry],
+            recv_sem=near_recv.at[4 * slot + 2 * h + kind],
+            device_id=device,
+            device_id_type=MESH,
+        )
+
+    def from_near(entry):
+        there, device, (start, size), slot, other, kind = receives[entry]
+        part = window.at[in_window(slot, other, start, size)]
+        return pltpu.make_async_remote_copy(
+            src_ref=part,
+            dst_ref=part,
+            send_sem=near_send.at[0],
+            recv_sem=near_recv.at[4 * slot + 2 * other + kind],
+            device_id=device,
+            device_id_type=MESH,
+        )
+
+    for entry in range(len(sends)):
+        where_there(sends[entry][0], lambda entry=entry: to_near(entry).start())
 
     tile_lane = lax.broadcasted_iota(jnp.int32, (8, LANES), 1)
     tile_line = lax.broadcasted_iota(jnp.int32, (8, LANES), 0)
@@ -383,31 +441,29 @@
             + smooth[2] * (z_sum - twice)
         )
 
-    for db, dk, there in near:
-
-        @pl.when(there)
-        def _():
-            to_near(-db, -dk).wait_recv()
+    for entry in range(len(receives)):
+        where_there(receives[entry][0], lambda entry=entry: from_near(entry).wait_recv())
 
     def tile(db, dk):
-        return masked if db == 0 and dk == 0 else around[(db + 1) * 3 + dk + 1]
+        return sum(window[in_window(db + 1, other, 8 * (dk + 1), 8), :] for other in range(2))
 
     empty = jnp.zeros((8, LANES), f32)
 
     def inside(there, value):
         return jnp.where(there, value, 0.0)
 
-    mid = one_pass(masked, tile(-1, 0), tile(1, 0), tile(0, -1), tile(0, 1))
-    prev = one_pass(tile(-1, 0), empty, masked, tile(-1, -1), tile(-1, 1))
-    after = one_pass(tile(1, 0), masked, empty, tile(1, -1), tile(1, 1))
-    lower = one_pass(tile(0, -1), tile(-1, -1), tile(1, -1), empty, masked)
-    upper = one_pass(tile(0, 1), tile(-1, 1), tile(1, 1), masked, empty)
+    middle = tile(0, 0)
+    mid = one_pass(middle, tile(-1, 0), tile(1, 0), tile(0, -1), tile(0, 1))
+    prev = one_pass(tile(-1, 0), empty, middle, tile(-1, -1), tile(-1, 1))
+    after = one_pass(tile(1, 0), middle, empty, tile(1, -1), tile(1, 1))
+    lower = one_pass(tile(0, -1), tile(-1, -1), tile(1, -1), empty, middle)
+    upper = one_pass(tile(0, 1), tile(-1, 1), tile(1, 1), middle, empty)
     out[...] = one_pass(
         mid,
         inside(has_prev, prev),
         inside(has_next, after),
-        inside(has_low, lower),
-        inside(has_high, upper),
+        inside(k > 0, lower),
+        inside(k < chunks - 1, upper),
     )
 
     def sent_halo(f, carry):
@@ -422,18 +478,17 @@
         return carry
 
     lax.fori_loop(0, count, sent_halo, 0)
+    to_partner(0).wait_send()
+    to_partner(1).wait_send()
     gathered.wait_send()
     scattered.wait_send()
-    for db, dk, there in near:
-
-        @pl.when(there)
-        def _():
-            to_near(db, dk).wait_send()
+    for entry in range(len(sends)):
+        where_there(sends[entry][0], lambda entry=entry: to_near(entry).wait_send())
 
 
 def solution(mesh):
-    n_src, n_freq, n_space = mesh.shape["src"], mesh.shape["freq"], mesh.shape["space"]
-    chunks = n_src * n_freq
+    n_src, n_space = mesh.shape["src"], mesh.shape["space"]
+    chunks = 2 * n_src
 
     def local(
         forward,
@@ -450,55 +505,55 @@
     ):
         count = forward.shape[1]
 
+        def keep(x):
+            return pltpu.with_memory_space_constraint(x, pltpu.HBM)
+
         def lines(field):
             split = field.reshape(count, 2, 2, chunks, LANES)
             return split.transpose(0, 1, 3, 2, 4).reshape(count, 4 * chunks, LANES)
 
-        any_spec = pl.BlockSpec(memory_space=pl.ANY)
+        hbm = pl.BlockSpec(memory_space=pl.ANY)
         vmem = pl.BlockSpec(memory_space=pltpu.VMEM)
         smem = pl.BlockSpec(memory_space=pltpu.SMEM)
         f32 = jnp.float32
         result = pl.pallas_call(
-            functools.partial(kernel, (n_src, n_freq, n_space, count)),
+            functools.partial(kernel, (n_src, n_space, count)),
             out_shape=jax.ShapeDtypeStruct((8, LANES), f32),
-            in_specs=[any_spec] * 2 + [vmem] * 5 + [smem] * 4,
+            in_specs=[hbm] * 7 + [smem] * 4,
             out_specs=vmem,
             scratch_shapes=[
+                pltpu.VMEM((4, 2, LANES), f32),
+                pltpu.VMEM((2, LANES), jnp.int32),
                 pltpu.VMEM((2, count, 4 * chunks, LANES), f32),
                 pltpu.VMEM((2, count, 4 * chunks, LANES), f32),
                 pltpu.VMEM((count, 4 * chunks, LANES), f32),
                 pltpu.VMEM((count, 4 * chunks, LANES), f32),
                 pltpu.VMEM((8 * chunks, LANES), f32),
+                pltpu.VMEM((16, LANES), f32),
                 pltpu.VMEM((8 * chunks, LANES), f32),
                 pltpu.VMEM((8 * chunks, LANES), f32),
-                pltpu.VMEM((8, LANES), f32),
-                pltpu.VMEM((9, 8, LANES), f32),
+                pltpu.VMEM((6 * 24, LANES), f32),
                 pltpu.VMEM((count, 2, 8, chunks, LANES), f32),
                 pltpu.VMEM((count, 2, 2, chunks, LANES), f32),
                 pltpu.VMEM((2, 4, chunks, LANES), f32),
                 pltpu.SemaphoreType.DMA((2,)),
+                pltpu.SemaphoreType.DMA((5,)),
                 pltpu.SemaphoreType.DMA((2, count)),
                 pltpu.SemaphoreType.DMA((2, count)),
                 pltpu.SemaphoreType.DMA((2,)),
                 pltpu.SemaphoreType.DMA((2,)),
-                pltpu.SemaphoreType.DMA((9,)),
-                pltpu.SemaphoreType.DMA((9,)),
+                pltpu.SemaphoreType.DMA((2,)),
+                pltpu.SemaphoreType.DMA((2,)),
+                pltpu.SemaphoreType.DMA((11,)),
+                pltpu.SemaphoreType.DMA((12,)),
             ],
             compiler_params=pltpu.CompilerParams(
                 collective_id=0, has_side_effects=True, vmem_limit_bytes=32 * 1024 * 1024
             ),
         )(
-            lines(forward),
-            lines(adjoint),
-            log_sigma,
-            charge,
-            log_tau,
-            exponent,
-            active,
+            *map(keep, (lines(forward), lines(adjoint), log_sigma, charge, log_tau, exponent, active)),
             source_group,
-            group_weight,
-            frequency_index,
-            prior_weight,
+            *map(keep, (group_weight, frequency_index, prior_weight)),
         )
         return result.reshape(4, 2, LANES)
 

time: 56.5 us -> 43.7 us (0.77)
  Pallas kernels: 50.2 us -> 42.2 us
  local copies, waits for them, and re-layouts: 5.26 us -> 0.6 us
    pallas_call x1, Pallas kernels: 50.2 us -> 42.2 us  [local(): pl.pallas_call(functools.partial(kernel, (n_src, n_space, count)), out_sh...]
    unnamed x21 -> x1, local copies, waits for them, and re-layouts: 5.26 us -> 0.6 us
where the time goes in v2:
time: 43.7 us; the launch traced here: 43.5 us
  Pallas kernels  42.2 us (97%)
  between operations  0.66 us (2%)
  local copies, waits for them, and re-layouts  0.6 us (1%)
    pallas_call x1, Pallas kernels, local(): pl.pallas_call(functools.partial(kernel, (n_src, n_space, count)), out_sh...  42.2 us

profile of v2, /device:TPU:1, one launch (start us, length us, event | category | flops | bytes accessed | tf_op | source)
XLA Modules:
  0.0 43.5 jit_solution(5261475892003554762)
XLA Ops:
  0.7 42.2 %shard_map.109 = f32[8,128]{1,0:T(8,128)S(1)} custom-call(f32[8,96,128]{2,1,0:T(8,128)} %bitcast.12, f32[8,96,128]{2,1,0:T(8,128)} %bitcast.13, f32[2,128]{1,0:T(2,128)} %log_sigma.1, f32[2,128]{1,0:T(2,128)} %charge.1, f32[2,128]{1,0:T(2,128)} %log_tau.1, f32[2,128]{1,0:T(2,128)} %exponent.1, s32[2,128]{1,0:T(2,128)} %active_in.1, s32[1]{0:T(128)S(6)} %copy.15.source_group, ...), custom_call_target="tpu_custom_call" | custom-call | tf_op jit(solution)/shard_map/pallas_call | solution.py:519
  42.9 0.6 %copy.16 = f32[4,2,128]{2,1,0:T(2,128)} copy(f32[4,2,128]{2,1,0:T(2,128)S(1)} %bitcast.11) | data formatting | bytes 8192

commit v3 on v2

--- a/solution.py
+++ b/solution.py
@@ -41,7 +41,7 @@
     window,
     derivs,
     yz_corr,
-    yz_grad,
+    log_omega,
     load_sem,
     small_sem,
     halo_send,
@@ -52,10 +52,15 @@
     scatter_sem,
     near_send,
     near_recv,
+    first_sem,
+    second_sem,
 ):
     n_src, n_space, count = sizes
     chunks = 2 * n_src
     half = 2 * chunks
+    size = min(8, chunks)
+    groups = chunks // size
+    places = size // 2
     s, h, b = lax.axis_index("src"), lax.axis_index("freq"), lax.axis_index("space")
     k = 2 * s + h
     f32 = jnp.float32
@@ -91,8 +96,8 @@
             return second if first is None else first
         return jnp.logical_and(first, second)
 
-    def in_window(slot, share, start, size):
-        return pl.ds(pl.multiple_of(48 * slot + 24 * share + start, 8), size)
+    def in_window(slot, share, start, length):
+        return pl.ds(pl.multiple_of(48 * slot + 24 * share + start, 8), length)
 
     def where_there(there, act):
         if there is None:
@@ -121,22 +126,30 @@
             there = both(has_side, beside[db])
             receives.append((there, (side, other, b + db), (16 * h, 8), 1 + db, other, 1))
 
+    odd = lax.rem(b, 2)
+    first_core, second_core = b - odd, b - odd + 1
+    next_chip = first_core - 2 + 4 * odd
+    has_chip = jnp.logical_and(next_chip >= 0, next_chip < n_space)
     barrier = pltpu.get_barrier_semaphore()
 
-    def greet(device):
+    def greet(*device):
         pl.semaphore_signal(barrier, inc=1, device_id=device, device_id_type=MESH)
 
-    for there, device, _, slot, other, kind in receives:
-        if kind == 1 and slot == 1 and other is h:
-            continue
-        where_there(there, functools.partial(greet, device))
+    where_there(odd == 1, functools.partial(greet, s, h, first_core))
+    where_there(has_chip, functools.partial(greet, s, h, next_chip))
+    greet(s, 1 - h, first_core)
+
+    where_there(both(has_side, has_chip), functools.partial(greet, side, 1 - h, next_chip + 1))
+    where_there(has_side, functools.partial(greet, side, 1 - h, second_core))
+    where_there(has_chip, functools.partial(greet, s, 1 - h, next_chip + 1))
     for step in steps:
-        greet((along(step), h, b))
-    one = jnp.int32(1)
-    sides = has_prev.astype(jnp.int32) + has_next.astype(jnp.int32)
-    expected = n_src - 1 + one + 2 * sides
-    expected = expected + has_side.astype(jnp.int32) * (1 + sides)
-    expected = expected + has_away.astype(jnp.int32) * sides
+        greet(along(step), h, second_core)
+    where_there(both(has_side, has_chip), functools.partial(greet, side, h, next_chip + 1))
+
+    chips = (first_core > 0).astype(jnp.int32) + (second_core < n_space - 1).astype(jnp.int32)
+    to_side, to_away = has_side.astype(jnp.int32), has_away.astype(jnp.int32)
+    first_count = 3 + chips
+    second_count = 2 * (n_src - 1) + chips * (1 + to_side + to_away) + 2 * to_side
 
     mine = pl.ds(pl.multiple_of(8 * k, 8), 8)
     my_half = pl.ds(pl.multiple_of(8 * h, 8), 8)
@@ -151,7 +164,9 @@
     def split_rows(f, carry):
         for i in range(2):
             for r in range(2):
-                rows[r, f, pl.ds(half * i, half), :] = own[i, f, pl.ds(r, half, stride=2), :]
+                for c in range(2):
+                    first = half * c + r
+                    rows[r, f, 2 * i + c] = own[i, f, pl.ds(first, chunks, stride=2), :]
         return carry
 
     lax.fori_loop(0, count, split_rows, 0)
@@ -172,7 +187,14 @@
             for other in range(2):
                 window[in_window(db, other, 16 * h, 8), :] = jnp.zeros((8, LANES), f32)
 
-    pl.semaphore_wait(barrier, expected)
+    @pl.when(odd == 0)
+    def _():
+        pl.semaphore_wait(barrier, first_count)
+        pl.semaphore_signal(first_sem, inc=1, device_id=(s, h, second_core), device_id_type=MESH)
+
+    @pl.when(odd == 1)
+    def _():
+        pl.semaphore_wait(first_sem, 1)
 
     def to_partner(i):
         ref, part = ((params, mine), (masks, my_half))[i]
@@ -187,38 +209,32 @@
 
     to_partner(0).start()
 
-    def up(f):
+    def part(g):
+        return pl.ds(size * g, size)
+
+    def up(g):
         return pltpu.make_async_remote_copy(
-            src_ref=rows.at[1, f],
-            dst_ref=from_prev.at[f],
-            send_sem=halo_send.at[0, f],
-            recv_sem=halo_recv.at[0, f],
+            src_ref=rows.at[1, :, :, part(g), :],
+            dst_ref=from_prev.at[:, :, part(g), :],
+            send_sem=halo_send.at[0, g],
+            recv_sem=halo_recv.at[0, g],
             device_id=(s, h, b + 1),
             device_id_type=MESH,
         )
 
-    def down(f):
+    def down(g):
         return pltpu.make_async_remote_copy(
-            src_ref=rows.at[0, f],
-            dst_ref=from_next.at[f],
-            send_sem=halo_send.at[1, f],
-            recv_sem=halo_recv.at[1, f],
+            src_ref=rows.at[0, :, :, part(g), :],
+            dst_ref=from_next.at[:, :, part(g), :],
+            send_sem=halo_send.at[1, g],
+            recv_sem=halo_recv.at[1, g],
             device_id=(s, h, b - 1),
             device_id_type=MESH,
         )
 
-    def send_halo(f, carry):
-        @pl.when(has_next)
-        def _():
-            up(f).start()
-
-        @pl.when(has_prev)
-        def _():
-            down(f).start()
-
-        return carry
-
-    lax.fori_loop(0, count, send_halo, 0)
+    for g in range(groups):
+        where_there(has_next, lambda g=g: up(g).start())
+        where_there(has_prev, lambda g=g: down(g).start())
     to_partner(1).start()
 
     lane = lax.broadcasted_iota(jnp.int32, (chunks, LANES), 1)
@@ -240,14 +256,23 @@
     def correlate_yz(f, carry):
         for r in range(2):
             grads = [
-                differences(rows[r, f, pl.ds(chunks * i, chunks), :]) for i in range(4)
+                differences(rows[r, f, i]) for i in range(4)
             ]
             (fr_y, fr_z), (fi_y, fi_z), (ar_y, ar_z), (ai_y, ai_z) = grads
-            yz_corr[f, r, 0] = fr_y * ar_y - fi_y * ai_y + (fr_z * ar_z - fi_z * ai_z)
-            yz_corr[f, r, 1] = fr_y * ai_y + fi_y * ar_y + (fr_z * ai_z + fi_z * ar_z)
+            yz_corr[r, 0, f] = fr_y * ar_y - fi_y * ai_y + (fr_z * ar_z - fi_z * ai_z)
+            yz_corr[r, 1, f] = fr_y * ai_y + fi_y * ar_y + (fr_z * ai_z + fi_z * ar_z)
         return carry
 
     lax.fori_loop(0, count, correlate_yz, 0)
+
+    @pl.when(odd == 1)
+    def _():
+        pl.semaphore_wait(barrier, second_count)
+        pl.semaphore_signal(second_sem, inc=1, device_id=(s, h, first_core), device_id_type=MESH)
+
+    @pl.when(odd == 0)
+    def _():
+        pl.semaphore_wait(second_sem, 1)
 
     to_partner(0).wait_recv()
     pair = pl.ds(pl.multiple_of(16 * s, 16), 16)
@@ -256,42 +281,48 @@
             src_ref=params.at[pair],
             dst_ref=params.at[pair],
             send_sem=gather_sem.at[0],
-            recv_sem=gather_sem.at[1],
+            recv_sem=gather_sem.at[1 + s // places],
             device_id=(along(step), h, b),
             device_id_type=MESH,
         ).start()
     others = pl.ds(0, 16 * (n_src - 1))
-    gathered = pltpu.make_async_remote_copy(
-        src_ref=partial.at[others],
-        dst_ref=params.at[others],
-        send_sem=gather_sem.at[0],
-        recv_sem=gather_sem.at[1],
-        device_id=(along(1), h, b),
-        device_id_type=MESH,
-    )
-    gathered.wait_recv()
+
+    def gathered(g, count_of):
+        there = pl.ds(0, 16 * count_of)
+        return pltpu.make_async_remote_copy(
+            src_ref=partial.at[there],
+            dst_ref=params.at[there],
+            send_sem=gather_sem.at[0],
+            recv_sem=gather_sem.at[1 + g],
+            device_id=(along(1), h, b),
+            device_id_type=MESH,
+        )
 
     weight = jnp.float32(0.0)
     for g in range(GROUPS):
         weight = weight + jnp.where(source_group[0] == g, group_weight[g], 0.0)
     scale = weight * (0.25 / math.sqrt(n_src * 2 * count))
 
-    for r in range(2):
-        sigma, chg, tau, expo = (
-            params[pl.ds(2 * p + r, chunks, stride=8), :] for p in range(4)
-        )
-        sigma = jnp.exp(sigma) * scale
-        angle = expo * (0.5 * math.pi)
-        cosine, sine = jnp.cos(angle), jnp.sin(angle)
-        rest = 1.0 - chg
-        q_scale = sigma * chg
-
-        def chain(f, totals):
-            index = frequency_index[h * count + f].astype(f32)
-            log_omega = math.log(2.0 * math.pi) + math.log(10.0) * (
-                -1.0 + (4.0 / (2 * count - 1)) * index
+    for f in range(count):
+        index = frequency_index[h * count + f].astype(f32)
+        value = math.log(2.0 * math.pi) + math.log(10.0) * (-1.0 + (4.0 / (2 * count - 1)) * index)
+        log_omega[f] = jnp.full((size, LANES), value, f32)
+
+    for g in range(groups):
+        inside_group = s // places == g
+        if places > 1:
+            where_there(inside_group, lambda g=g: gathered(g, places - 1).wait_recv())
+        where_there(jnp.logical_not(inside_group), lambda g=g: gathered(g, places).wait_recv())
+        for r in range(2):
+            sigma, chg, tau, expo = (
+                params[pl.ds(8 * size * g + 2 * p + r, size, stride=8), :] for p in range(4)
             )
-            log_product = log_omega + tau
+            sigma = jnp.exp(sigma) * scale
+            angle = expo * (0.5 * math.pi)
+            cosine, sine = jnp.cos(angle), jnp.sin(angle)
+            rest = 1.0 - chg
+            q_scale = sigma * chg
+            log_product = log_omega[...] + tau
             amplitude = jnp.exp(expo * log_product)
             z_r, z_i = amplitude * cosine, amplitude * sine
             d_r, d_i = 1.0 + rest * z_r, rest * z_i
@@ -310,60 +341,38 @@
                     (0.5 * math.pi) * q_r + q_i * log_product,
                 ),
             )
-            c_r, c_i = yz_corr[f, r, 0], yz_corr[f, r, 1]
-            new = []
             for p, (part_r, part_i) in enumerate(parts):
-                derivs[f, r, 2 * p] = part_r
-                derivs[f, r, 2 * p + 1] = part_i
-                new.append(totals[p] + (part_r * c_r - part_i * c_i))
-            return tuple(new)
-
-        zeros = jnp.zeros((chunks, LANES), f32)
-        totals = lax.fori_loop(0, count, chain, (zeros,) * 4)
-        for p in range(4):
-            yz_grad[r, p] = totals[p]
-
-    def add_x(f, totals):
-        @pl.when(has_prev)
-        def _():
-            up(f).wait_recv()
-
-        @pl.when(has_next)
-        def _():
-            down(f).wait_recv()
-
-        new = []
+                derivs[r, 2 * p] = part_r
+                derivs[r, 2 * p + 1] = part_i
+
+        where_there(has_prev, lambda g=g: up(g).wait_recv())
+        where_there(has_next, lambda g=g: down(g).wait_recv())
         for r in range(2):
-            ahead = rows.at[1, f] if r == 0 else from_next.at[f]
-            behind = from_prev.at[f] if r == 0 else rows.at[0, f]
+            ahead = rows.at[1] if r == 0 else from_next
+            behind = from_prev if r == 0 else rows.at[0]
             f_r, f_i, a_r, a_i = (
-                ahead[pl.ds(chunks * i, chunks), :] - behind[pl.ds(chunks * i, chunks), :]
-                for i in range(4)
+                ahead[:, i, part(g), :] - behind[:, i, part(g), :] for i in range(4)
             )
-            c_r, c_i = f_r * a_r - f_i * a_i, f_r * a_i + f_i * a_r
+            c_r = f_r * a_r - f_i * a_i + yz_corr[r, 0, :, part(g), :]
+            c_i = f_r * a_i + f_i * a_r + yz_corr[r, 1, :, part(g), :]
             for p in range(4):
-                new.append(
-                    totals[4 * r + p] + (derivs[f, r, 2 * p] * c_r - derivs[f, r, 2 * p + 1] * c_i)
-                )
-        return tuple(new)
-
-    totals = lax.fori_loop(
-        0, count, add_x, tuple(yz_grad[r, p] for r in range(2) for p in range(4))
-    )
-    for r in range(2):
-        for p in range(4):
-            partial[pl.ds(2 * p + r, chunks, stride=8), :] = totals[4 * r + p]
-
-    for i, step in enumerate(steps):
-        to = along(step)
-        pltpu.make_async_remote_copy(
-            src_ref=partial.at[pl.ds(pl.multiple_of(16 * to, 16), 16)],
-            dst_ref=arrived.at[pl.ds(16 * i, 16)],
-            send_sem=scatter_sem.at[0],
-            recv_sem=scatter_sem.at[1],
-            device_id=(to, h, b),
-            device_id_type=MESH,
-        ).start()
+                gradient = jnp.sum(derivs[r, 2 * p] * c_r - derivs[r, 2 * p + 1] * c_i, axis=0)
+                partial[pl.ds(8 * size * g + 2 * p + r, size, stride=8), :] = gradient
+
+        for i in range(places):
+            to = places * g + lax.rem(s + i, places)
+
+            @pl.when(s != to)
+            def _():
+                pltpu.make_async_remote_copy(
+                    src_ref=partial.at[pl.ds(pl.multiple_of(16 * to, 16), 16)],
+                    dst_ref=arrived.at[pair],
+                    send_sem=scatter_sem.at[0],
+                    recv_sem=scatter_sem.at[1],
+                    device_id=(to, h, b),
+                    device_id_type=MESH,
+                ).start()
+
     to_partner(1).wait_recv()
     mask = masks[...]
     scattered = pltpu.make_async_remote_copy(
@@ -375,7 +384,8 @@
         device_id_type=MESH,
     )
     scattered.wait_recv()
-    tiles = [partial[pair, :]] + [arrived[pl.ds(16 * i, 16), :] for i in range(n_src - 1)]
+    arrived[pair, :] = partial[pair, :]
+    tiles = [arrived[pl.ds(16 * i, 16), :] for i in range(n_src)]
     while len(tiles) > 1:
         tiles = [
             tiles[i] + tiles[i + 1] if i + 1 < len(tiles) else tiles[i]
@@ -384,10 +394,10 @@
     window[in_window(1, h, 8 - 8 * h, 16), :] = tiles[0] * mask
 
     def to_near(entry):
-        there, part, device, (start, size), slot, kind = sends[entry]
+        there, part, device, (start, length), slot, kind = sends[entry]
         return pltpu.make_async_remote_copy(
-            src_ref=window.at[in_window(1, h, 8 - 8 * h + part, size)],
-            dst_ref=window.at[in_window(slot, h, start, size)],
+            src_ref=window.at[in_window(1, h, 8 - 8 * h + part, length)],
+            dst_ref=window.at[in_window(slot, h, start, length)],
             send_sem=near_send.at[entry],
             recv_sem=near_recv.at[4 * slot + 2 * h + kind],
             device_id=device,
@@ -395,8 +405,8 @@
         )
 
     def from_near(entry):
-        there, device, (start, size), slot, other, kind = receives[entry]
-        part = window.at[in_window(slot, other, start, size)]
+        there, device, (start, length), slot, other, kind = receives[entry]
+        part = window.at[in_window(slot, other, start, length)]
         return pltpu.make_async_remote_copy(
             src_ref=part,
             dst_ref=part,
@@ -466,21 +476,12 @@
         inside(k < chunks - 1, upper),
     )
 
-    def sent_halo(f, carry):
-        @pl.when(has_next)
-        def _():
-            up(f).wait_send()
-
-        @pl.when(has_prev)
-        def _():
-            down(f).wait_send()
-
-        return carry
-
-    lax.fori_loop(0, count, sent_halo, 0)
+    for g in range(groups):
+        where_there(has_next, lambda g=g: up(g).wait_send())
+        where_there(has_prev, lambda g=g: down(g).wait_send())
     to_partner(0).wait_send()
     to_partner(1).wait_send()
-    gathered.wait_send()
+    gathered(0, n_src - 1).wait_send()
     scattered.wait_send()
     for entry in range(len(sends)):
         where_there(sends[entry][0], lambda entry=entry: to_near(entry).wait_send())
@@ -504,6 +505,8 @@
         prior_weight,
     ):
         count = forward.shape[1]
+        size = min(8, chunks)
+        groups = chunks // size
 
         def keep(x):
             return pltpu.with_memory_space_constraint(x, pltpu.HBM)
@@ -525,27 +528,29 @@
                 pltpu.VMEM((4, 2, LANES), f32),
                 pltpu.VMEM((2, LANES), jnp.int32),
                 pltpu.VMEM((2, count, 4 * chunks, LANES), f32),
-                pltpu.VMEM((2, count, 4 * chunks, LANES), f32),
-                pltpu.VMEM((count, 4 * chunks, LANES), f32),
-                pltpu.VMEM((count, 4 * chunks, LANES), f32),
+                pltpu.VMEM((2, count, 4, chunks, LANES), f32),
+                pltpu.VMEM((count, 4, chunks, LANES), f32),
+                pltpu.VMEM((count, 4, chunks, LANES), f32),
                 pltpu.VMEM((8 * chunks, LANES), f32),
                 pltpu.VMEM((16, LANES), f32),
                 pltpu.VMEM((8 * chunks, LANES), f32),
                 pltpu.VMEM((8 * chunks, LANES), f32),
                 pltpu.VMEM((6 * 24, LANES), f32),
-                pltpu.VMEM((count, 2, 8, chunks, LANES), f32),
-                pltpu.VMEM((count, 2, 2, chunks, LANES), f32),
-                pltpu.VMEM((2, 4, chunks, LANES), f32),
+                pltpu.VMEM((2, 8, count, size, LANES), f32),
+                pltpu.VMEM((2, 2, count, chunks, LANES), f32),
+                pltpu.VMEM((count, size, LANES), f32),
                 pltpu.SemaphoreType.DMA((2,)),
                 pltpu.SemaphoreType.DMA((5,)),
-                pltpu.SemaphoreType.DMA((2, count)),
-                pltpu.SemaphoreType.DMA((2, count)),
+                pltpu.SemaphoreType.DMA((2, groups)),
+                pltpu.SemaphoreType.DMA((2, groups)),
                 pltpu.SemaphoreType.DMA((2,)),
                 pltpu.SemaphoreType.DMA((2,)),
-                pltpu.SemaphoreType.DMA((2,)),
+                pltpu.SemaphoreType.DMA((1 + groups,)),
                 pltpu.SemaphoreType.DMA((2,)),
                 pltpu.SemaphoreType.DMA((11,)),
                 pltpu.SemaphoreType.DMA((12,)),
+                pltpu.SemaphoreType.REGULAR,
+                pltpu.SemaphoreType.REGULAR,
             ],
             compiler_params=pltpu.CompilerParams(
                 collective_id=0, has_side_effects=True, vmem_limit_bytes=32 * 1024 * 1024

time: 43.7 us -> 39 us (0.89)
  Pallas kernels: 42.2 us -> 37.6 us
    pallas_call x1, Pallas kernels: 42.2 us -> 37.6 us  [local(): pl.pallas_call(functools.partial(kernel, (n_src, n_space, count)), out_sh...]
where the time goes in v3:
time: 39 us; the launch traced here: 38.8 us
  Pallas kernels  37.6 us (96%)
  between operations  0.66 us (2%)
  local copies, waits for them, and re-layouts  0.6 us (2%)
    pallas_call x1, Pallas kernels, local(): pl.pallas_call(functools.partial(kernel, (n_src, n_space, count)), out_sh...  37.6 us

profile of v3, /device:TPU:1, one launch (start us, length us, event | category | flops | bytes accessed | tf_op | source)
XLA Modules:
  0.0 38.8 jit_solution(5427919453990148497)
XLA Ops:
  0.7 37.6 %shard_map.109 = f32[8,128]{1,0:T(8,128)S(1)} custom-call(f32[8,96,128]{2,1,0:T(8,128)} %bitcast.12, f32[8,96,128]{2,1,0:T(8,128)} %bitcast.13, f32[2,128]{1,0:T(2,128)} %log_sigma.1, f32[2,128]{1,0:T(2,128)} %charge.1, f32[2,128]{1,0:T(2,128)} %log_tau.1, f32[2,128]{1,0:T(2,128)} %exponent.1, s32[2,128]{1,0:T(2,128)} %active_in.1, s32[1]{0:T(128)S(6)} %copy.15.source_group, ...), custom_call_target="tpu_custom_call" | custom-call | tf_op jit(solution)/shard_map/pallas_call | solution.py:522
  38.2 0.6 %copy.16 = f32[4,2,128]{2,1,0:T(2,128)} copy(f32[4,2,128]{2,1,0:T(2,128)S(1)} %bitcast.11) | data formatting | bytes 8192

commit v4 on v3

--- a/solution.py
+++ b/solution.py
@@ -24,12 +24,15 @@
     exponent,
     active_in,
     source_group,
+    group_weight_in,
+    frequency_index_in,
+    prior_weight_in,
+    out,
+    cell_params,
+    active,
     group_weight,
     frequency_index,
     prior_weight,
-    out,
-    cell_params,
-    active,
     own,
     rows,
     from_prev,
@@ -82,12 +85,12 @@
                 (log_tau, cell_params.at[2]),
                 (exponent, cell_params.at[3]),
                 (active_in, active),
+                (group_weight_in, group_weight),
+                (frequency_index_in, frequency_index),
+                (prior_weight_in, prior_weight),
             )
         )
     ]
-    for load in loads + small:
-        load.start()
-
     has_prev, has_next = b > 0, b < n_space - 1
     beside = {-1: has_prev, 0: None, 1: has_next}
 
@@ -109,14 +112,15 @@
     has_side = jnp.logical_and(side >= 0, side < n_src)
     has_away = jnp.logical_and(away >= 0, away < n_src)
     sends = []
-    for db in (-1, 0, 1):
+    for db in (-1, 1, 0):
+        there = both(has_side, beside[db])
+        sends.append((there, 8 * h, (side, 1 - h, b + db), (16 - 16 * h, 8), 1 - db, 1))
+        sends.append((beside[db], 0, (s, 1 - h, b + db), (8 * h, 16), 1 - db, 0))
+    for db in (-1, 1, 0):
+        there = both(has_away, beside[db])
+        sends.append((there, 8 - 8 * h, (away, h, b + db), (16 * h, 8), 1 - db, 1))
         if db != 0:
             sends.append((beside[db], 0, (s, h, b + db), (8 - 8 * h, 16), 1 - db, 0))
-        sends.append((beside[db], 0, (s, 1 - h, b + db), (8 * h, 16), 1 - db, 0))
-        there = both(has_away, beside[db])
-        sends.append((there, 8 - 8 * h, (away, h, b + db), (16 * h, 8), 1 - db, 1))
-        there = both(has_side, beside[db])
-        sends.append((there, 8 * h, (side, 1 - h, b + db), (16 - 16 * h, 8), 1 - db, 1))
     receives = []
     for db in (-1, 0, 1):
         if db != 0:
@@ -135,15 +139,16 @@
     def greet(*device):
         pl.semaphore_signal(barrier, inc=1, device_id=device, device_id_type=MESH)
 
+    for step in steps:
+        greet(along(step), h, second_core)
     where_there(odd == 1, functools.partial(greet, s, h, first_core))
     where_there(has_chip, functools.partial(greet, s, h, next_chip))
     greet(s, 1 - h, first_core)
-
+    for load in loads + small:
+        load.start()
     where_there(both(has_side, has_chip), functools.partial(greet, side, 1 - h, next_chip + 1))
     where_there(has_side, functools.partial(greet, side, 1 - h, second_core))
     where_there(has_chip, functools.partial(greet, s, 1 - h, next_chip + 1))
-    for step in steps:
-        greet(along(step), h, second_core)
     where_there(both(has_side, has_chip), functools.partial(greet, side, h, next_chip + 1))
 
     chips = (first_core > 0).astype(jnp.int32) + (second_core < n_space - 1).astype(jnp.int32)
@@ -451,6 +456,14 @@
             + smooth[2] * (z_sum - twice)
         )
 
+    for g in range(groups):
+        where_there(has_next, lambda g=g: up(g).wait_send())
+        where_there(has_prev, lambda g=g: down(g).wait_send())
+    to_partner(0).wait_send()
+    to_partner(1).wait_send()
+    gathered(0, n_src - 1).wait_send()
+    scattered.wait_send()
+
     for entry in range(len(receives)):
         where_there(receives[entry][0], lambda entry=entry: from_near(entry).wait_recv())
 
@@ -476,13 +489,6 @@
         inside(k < chunks - 1, upper),
     )
 
-    for g in range(groups):
-        where_there(has_next, lambda g=g: up(g).wait_send())
-        where_there(has_prev, lambda g=g: down(g).wait_send())
-    to_partner(0).wait_send()
-    to_partner(1).wait_send()
-    gathered(0, n_src - 1).wait_send()
-    scattered.wait_send()
     for entry in range(len(sends)):
         where_there(sends[entry][0], lambda entry=entry: to_near(entry).wait_send())
 
@@ -522,11 +528,14 @@
         result = pl.pallas_call(
             functools.partial(kernel, (n_src, n_space, count)),
             out_shape=jax.ShapeDtypeStruct((8, LANES), f32),
-            in_specs=[hbm] * 7 + [smem] * 4,
+            in_specs=[hbm] * 7 + [smem] + [hbm] * 3,
             out_specs=vmem,
             scratch_shapes=[
                 pltpu.VMEM((4, 2, LANES), f32),
                 pltpu.VMEM((2, LANES), jnp.int32),
+                pltpu.SMEM(group_weight.shape, f32),
+                pltpu.SMEM(frequency_index.shape, jnp.int32),
+                pltpu.SMEM(prior_weight.shape, f32),
                 pltpu.VMEM((2, count, 4 * chunks, LANES), f32),
                 pltpu.VMEM((2, count, 4, chunks, LANES), f32),
                 pltpu.VMEM((count, 4, chunks, LANES), f32),
@@ -540,7 +549,7 @@
                 pltpu.VMEM((2, 2, count, chunks, LANES), f32),
                 pltpu.VMEM((count, size, LANES), f32),
                 pltpu.SemaphoreType.DMA((2,)),
-                pltpu.SemaphoreType.DMA((5,)),
+                pltpu.SemaphoreType.DMA((8,)),
                 pltpu.SemaphoreType.DMA((2, groups)),
                 pltpu.SemaphoreType.DMA((2, groups)),
                 pltpu.SemaphoreType.DMA((2,)),

time: 39 us -> 38 us (0.974)
  Pallas kernels: 37.6 us -> 36.6 us
    pallas_call x1, Pallas kernels: 37.6 us -> 36.6 us  [local(): pl.pallas_call(functools.partial(kernel, (n_src, n_space, count)), out_sh...]
where the time goes in v4:
time: 38 us; the launch traced here: 37.8 us
  Pallas kernels  36.6 us (96%)
  between operations  0.66 us (2%)
  local copies, waits for them, and re-layouts  0.6 us (2%)
    pallas_call x1, Pallas kernels, local(): pl.pallas_call(functools.partial(kernel, (n_src, n_space, count)), out_sh...  36.6 us

profile of v4, /device:TPU:1, one launch (start us, length us, event | category | flops | bytes accessed | tf_op | source)
XLA Modules:
  0.0 37.8 jit_solution(1615356431328037046)
XLA Ops:
  0.7 36.6 %shard_map.109 = f32[8,128]{1,0:T(8,128)S(1)} custom-call(f32[8,96,128]{2,1,0:T(8,128)} %bitcast.12, f32[8,96,128]{2,1,0:T(8,128)} %bitcast.13, f32[2,128]{1,0:T(2,128)} %log_sigma.1, f32[2,128]{1,0:T(2,128)} %charge.1, f32[2,128]{1,0:T(2,128)} %log_tau.1, f32[2,128]{1,0:T(2,128)} %exponent.1, s32[2,128]{1,0:T(2,128)} %active_in.1, s32[1]{0:T(128)S(6)} %copy.15.source_group, ...), custom_call_target="tpu_custom_call" | custom-call | tf_op jit(solution)/shard_map/pallas_call | solution.py:528
  37.2 0.6 %copy.16 = f32[4,2,128]{2,1,0:T(2,128)} copy(f32[4,2,128]{2,1,0:T(2,128)S(1)} %bitcast.11) | data formatting | bytes 8192

commit v5 on v4

--- a/solution.py
+++ b/solution.py
@@ -122,13 +122,14 @@
         if db != 0:
             sends.append((beside[db], 0, (s, h, b + db), (8 - 8 * h, 16), 1 - db, 0))
     receives = []
-    for db in (-1, 0, 1):
-        if db != 0:
-            receives.append((beside[db], (s, h, b + db), (8 - 8 * h, 16), 1 + db, h, 0))
-        receives.append((beside[db], (s, 1 - h, b + db), (8 - 8 * h, 16), 1 + db, 1 - h, 0))
-        for other in (h, 1 - h):
+    for db in (-1, 1):
+        receives.append((beside[db], (s, h, b + db), (8 - 8 * h, 16), 1 + db, h, 0))
+    for other in (h, 1 - h):
+        for db in (0, -1, 1):
             there = both(has_side, beside[db])
             receives.append((there, (side, other, b + db), (16 * h, 8), 1 + db, other, 1))
+    for db in (-1, 1, 0):
+        receives.append((beside[db], (s, 1 - h, b + db), (8 - 8 * h, 16), 1 + db, 1 - h, 0))
 
     odd = lax.rem(b, 2)
     first_core, second_core = b - odd, b - odd + 1
@@ -313,56 +314,81 @@
         value = math.log(2.0 * math.pi) + math.log(10.0) * (-1.0 + (4.0 / (2 * count - 1)) * index)
         log_omega[f] = jnp.full((size, LANES), value, f32)
 
+    def chain_rule(g, r):
+        sigma, chg, tau, expo = (
+            params[pl.ds(8 * size * g + 2 * p + r, size, stride=8), :] for p in range(4)
+        )
+        sigma = jnp.exp(sigma) * scale
+        angle = expo * (0.5 * math.pi)
+        cosine, sine = jnp.cos(angle), jnp.sin(angle)
+        rest = 1.0 - chg
+        q_scale = sigma * chg
+        log_product = log_omega[...] + tau
+        amplitude = jnp.exp(expo * log_product)
+        z_r, z_i = amplitude * cosine, amplitude * sine
+        d_r, d_i = 1.0 + rest * z_r, rest * z_i
+        inverse = 1.0 / (d_r * d_r + d_i * d_i)
+        r_r, r_i = d_r * inverse, -d_i * inverse
+        s_r, s_i = (1.0 + z_r) * r_r - z_i * r_i, (1.0 + z_r) * r_i + z_i * r_r
+        t_r, t_i = z_r * r_r - z_i * r_i, z_r * r_i + z_i * r_r
+        s_r, s_i = sigma * s_r, sigma * s_i
+        q_r, q_i = q_scale * (t_r * r_r - t_i * r_i), q_scale * (t_r * r_i + t_i * r_r)
+        parts = (
+            (s_r, s_i),
+            (s_r * t_r - s_i * t_i, s_r * t_i + s_i * t_r),
+            (expo * q_r, expo * q_i),
+            (
+                q_r * log_product - (0.5 * math.pi) * q_i,
+                (0.5 * math.pi) * q_r + q_i * log_product,
+            ),
+        )
+        return parts
+
+    def with_x(g, r):
+        ahead = rows.at[1] if r == 0 else from_next
+        behind = from_prev if r == 0 else rows.at[0]
+        f_r, f_i, a_r, a_i = (
+            ahead[:, i, part(g), :] - behind[:, i, part(g), :] for i in range(4)
+        )
+        c_r = f_r * a_r - f_i * a_i + yz_corr[r, 0, :, part(g), :]
+        c_i = f_r * a_i + f_i * a_r + yz_corr[r, 1, :, part(g), :]
+        return c_r, c_i
+
     for g in range(groups):
         inside_group = s // places == g
-        if places > 1:
-            where_there(inside_group, lambda g=g: gathered(g, places - 1).wait_recv())
-        where_there(jnp.logical_not(inside_group), lambda g=g: gathered(g, places).wait_recv())
+        def wait_params(g=g, inside_group=inside_group):
+            if places > 1:
+                where_there(inside_group, lambda g=g: gathered(g, places - 1).wait_recv())
+            where_there(jnp.logical_not(inside_group), lambda g=g: gathered(g, places).wait_recv())
+
+        def wait_rows(g=g):
+            where_there(has_prev, lambda g=g: up(g).wait_recv())
+            where_there(has_next, lambda g=g: down(g).wait_recv())
+
+        if g == 0:
+            wait_rows()
+            for r in range(2):
+                c_r, c_i = with_x(g, r)
+                yz_corr[r, 0, :, part(g), :], yz_corr[r, 1, :, part(g), :] = c_r, c_i
+        wait_params()
         for r in range(2):
-            sigma, chg, tau, expo = (
-                params[pl.ds(8 * size * g + 2 * p + r, size, stride=8), :] for p in range(4)
-            )
-            sigma = jnp.exp(sigma) * scale
-            angle = expo * (0.5 * math.pi)
-            cosine, sine = jnp.cos(angle), jnp.sin(angle)
-            rest = 1.0 - chg
-            q_scale = sigma * chg
-            log_product = log_omega[...] + tau
-            amplitude = jnp.exp(expo * log_product)
-            z_r, z_i = amplitude * cosine, amplitude * sine
-            d_r, d_i = 1.0 + rest * z_r, rest * z_i
-            inverse = 1.0 / (d_r * d_r + d_i * d_i)
-            r_r, r_i = d_r * inverse, -d_i * inverse
-            s_r, s_i = (1.0 + z_r) * r_r - z_i * r_i, (1.0 + z_r) * r_i + z_i * r_r
-            t_r, t_i = z_r * r_r - z_i * r_i, z_r * r_i + z_i * r_r
-            s_r, s_i = sigma * s_r, sigma * s_i
-            q_r, q_i = q_scale * (t_r * r_r - t_i * r_i), q_scale * (t_r * r_i + t_i * r_r)
-            parts = (
-                (s_r, s_i),
-                (s_r * t_r - s_i * t_i, s_r * t_i + s_i * t_r),
-                (expo * q_r, expo * q_i),
-                (
-                    q_r * log_product - (0.5 * math.pi) * q_i,
-                    (0.5 * math.pi) * q_r + q_i * log_product,
-                ),
-            )
-            for p, (part_r, part_i) in enumerate(parts):
-                derivs[r, 2 * p] = part_r
-                derivs[r, 2 * p + 1] = part_i
-
-        where_there(has_prev, lambda g=g: up(g).wait_recv())
-        where_there(has_next, lambda g=g: down(g).wait_recv())
-        for r in range(2):
-            ahead = rows.at[1] if r == 0 else from_next
-            behind = from_prev if r == 0 else rows.at[0]
-            f_r, f_i, a_r, a_i = (
-                ahead[:, i, part(g), :] - behind[:, i, part(g), :] for i in range(4)
-            )
-            c_r = f_r * a_r - f_i * a_i + yz_corr[r, 0, :, part(g), :]
-            c_i = f_r * a_i + f_i * a_r + yz_corr[r, 1, :, part(g), :]
-            for p in range(4):
-                gradient = jnp.sum(derivs[r, 2 * p] * c_r - derivs[r, 2 * p + 1] * c_i, axis=0)
-                partial[pl.ds(8 * size * g + 2 * p + r, size, stride=8), :] = gradient
+            parts = chain_rule(g, r)
+            if g == 0:
+                c_r, c_i = yz_corr[r, 0, :, part(g), :], yz_corr[r, 1, :, part(g), :]
+                for p, (part_r, part_i) in enumerate(parts):
+                    gradient = jnp.sum(part_r * c_r - part_i * c_i, axis=0)
+                    partial[pl.ds(8 * size * g + 2 * p + r, size, stride=8), :] = gradient
+            else:
+                for p, (part_r, part_i) in enumerate(parts):
+                    derivs[r, 2 * p] = part_r
+                    derivs[r, 2 * p + 1] = part_i
+        if g > 0:
+            wait_rows()
+            for r in range(2):
+                c_r, c_i = with_x(g, r)
+                for p in range(4):
+                    gradient = jnp.sum(derivs[r, 2 * p] * c_r - derivs[r, 2 * p + 1] * c_i, axis=0)
+                    partial[pl.ds(8 * size * g + 2 * p + r, size, stride=8), :] = gradient
 
         for i in range(places):
             to = places * g + lax.rem(s + i, places)
@@ -464,6 +490,9 @@
     gathered(0, n_src - 1).wait_send()
     scattered.wait_send()
 
+    for entry in range(len(sends)):
+        where_there(sends[entry][0], lambda entry=entry: to_near(entry).wait_send())
+
     for entry in range(len(receives)):
         where_there(receives[entry][0], lambda entry=entry: from_near(entry).wait_recv())
 
@@ -488,9 +517,6 @@
         inside(k > 0, lower),
         inside(k < chunks - 1, upper),
     )
-
-    for entry in range(len(sends)):
-        where_there(sends[entry][0], lambda entry=entry: to_near(entry).wait_send())
 
 
 def solution(mesh):

time: 38 us -> 38 us (level)
  no operation moved by 1% of the time
where the time goes in v5:
time: 38 us; the launch traced here: 37.8 us
  Pallas kernels  36.6 us (96%)
  between operations  0.66 us (2%)
  local copies, waits for them, and re-layouts  0.6 us (2%)
    pallas_call x1, Pallas kernels, local(): pl.pallas_call(functools.partial(kernel, (n_src, n_space, count)), out_sh...  36.6 us

profile of v5, /device:TPU:1, one launch (start us, length us, event | category | flops | bytes accessed | tf_op | source)
XLA Modules:
  0.0 37.8 jit_solution(11533890452374157291)
XLA Ops:
  0.7 36.6 %shard_map.109 = f32[8,128]{1,0:T(8,128)S(1)} custom-call(f32[8,96,128]{2,1,0:T(8,128)} %bitcast.12, f32[8,96,128]{2,1,0:T(8,128)} %bitcast.13, f32[2,128]{1,0:T(2,128)} %log_sigma.1, f32[2,128]{1,0:T(2,128)} %charge.1, f32[2,128]{1,0:T(2,128)} %log_tau.1, f32[2,128]{1,0:T(2,128)} %exponent.1, s32[2,128]{1,0:T(2,128)} %active_in.1, s32[1]{0:T(128)S(6)} %copy.15.source_group, ...), custom_call_target="tpu_custom_call" | custom-call | tf_op jit(solution)/shard_map/pallas_call | solution.py:554
  37.2 0.6 %copy.16 = f32[4,2,128]{2,1,0:T(2,128)} copy(f32[4,2,128]{2,1,0:T(2,128)S(1)} %bitcast.11) | data formatting | bytes 8192

commit v6 on v5

--- a/solution.py
+++ b/solution.py
@@ -73,7 +73,7 @@
         return lax.rem(s + step, n_src)
 
     loads = [
-        pltpu.make_async_copy(field, own.at[i], load_sem.at[i])
+        pltpu.make_async_copy(field, own.at[i, :, pl.ds(0, 2 * half), :], load_sem.at[i])
         for i, field in enumerate((forward, adjoint))
     ]
     small = [
@@ -562,13 +562,13 @@
                 pltpu.SMEM(group_weight.shape, f32),
                 pltpu.SMEM(frequency_index.shape, jnp.int32),
                 pltpu.SMEM(prior_weight.shape, f32),
-                pltpu.VMEM((2, count, 4 * chunks, LANES), f32),
+                pltpu.VMEM((2, count, 4 * chunks + 8, LANES), f32),
                 pltpu.VMEM((2, count, 4, chunks, LANES), f32),
                 pltpu.VMEM((count, 4, chunks, LANES), f32),
                 pltpu.VMEM((count, 4, chunks, LANES), f32),
-                pltpu.VMEM((8 * chunks, LANES), f32),
+                pltpu.VMEM((8 * chunks + 8, LANES), f32),
                 pltpu.VMEM((16, LANES), f32),
-                pltpu.VMEM((8 * chunks, LANES), f32),
+                pltpu.VMEM((8 * chunks + 8, LANES), f32),
                 pltpu.VMEM((8 * chunks, LANES), f32),
                 pltpu.VMEM((6 * 24, LANES), f32),
                 pltpu.VMEM((2, 8, count, size, LANES), f32),

time: 38 us -> 38 us (level)
  no operation moved by 1% of the time
where the time goes in v6:
time: 38 us; the launch traced here: 37.8 us
  Pallas kernels  36.6 us (96%)
  between operations  0.66 us (2%)
  local copies, waits for them, and re-layouts  0.6 us (2%)
    pallas_call x1, Pallas kernels, local(): pl.pallas_call(functools.partial(kernel, (n_src, n_space, count)), out_sh...  36.6 us

profile of v6, /device:TPU:1, one launch (start us, length us, event | category | flops | bytes accessed | tf_op | source)
XLA Modules:
  0.0 37.8 jit_solution(3243489631737627001)
XLA Ops:
  0.7 36.6 %shard_map.109 = f32[8,128]{1,0:T(8,128)S(1)} custom-call(f32[8,96,128]{2,1,0:T(8,128)} %bitcast.12, f32[8,96,128]{2,1,0:T(8,128)} %bitcast.13, f32[2,128]{1,0:T(2,128)} %log_sigma.1, f32[2,128]{1,0:T(2,128)} %charge.1, f32[2,128]{1,0:T(2,128)} %log_tau.1, f32[2,128]{1,0:T(2,128)} %exponent.1, s32[2,128]{1,0:T(2,128)} %active_in.1, s32[1]{0:T(128)S(6)} %copy.15.source_group, ...), custom_call_target="tpu_custom_call" | custom-call | tf_op jit(solution)/shard_map/pallas_call | solution.py:554
  37.2 0.6 %copy.16 = f32[4,2,128]{2,1,0:T(2,128)} copy(f32[4,2,128]{2,1,0:T(2,128)S(1)} %bitcast.11) | data formatting | bytes 8192

commit v7 on v6

--- a/solution.py
+++ b/solution.py
@@ -271,6 +271,16 @@
 
     lax.fori_loop(0, count, correlate_yz, 0)
 
+    weight = jnp.float32(0.0)
+    for g in range(GROUPS):
+        weight = weight + jnp.where(source_group[0] == g, group_weight[g], 0.0)
+    scale = weight * (0.25 / math.sqrt(n_src * 2 * count))
+
+    for f in range(count):
+        index = frequency_index[h * count + f].astype(f32)
+        value = math.log(2.0 * math.pi) + math.log(10.0) * (-1.0 + (4.0 / (2 * count - 1)) * index)
+        log_omega[f] = jnp.full((size, LANES), value, f32)
+
     @pl.when(odd == 1)
     def _():
         pl.semaphore_wait(barrier, second_count)
@@ -303,16 +313,6 @@
             device_id=(along(1), h, b),
             device_id_type=MESH,
         )
-
-    weight = jnp.float32(0.0)
-    for g in range(GROUPS):
-        weight = weight + jnp.where(source_group[0] == g, group_weight[g], 0.0)
-    scale = weight * (0.25 / math.sqrt(n_src * 2 * count))
-
-    for f in range(count):
-        index = frequency_index[h * count + f].astype(f32)
-        value = math.log(2.0 * math.pi) + math.log(10.0) * (-1.0 + (4.0 / (2 * count - 1)) * index)
-        log_omega[f] = jnp.full((size, LANES), value, f32)
 
     def chain_rule(g, r):
         sigma, chg, tau, expo = (

time: 38 us -> 38 us (level)
  no operation moved by 1% of the time
where the time goes in v7:
time: 38 us; the launch traced here: 37.8 us
  Pallas kernels  36.6 us (96%)
  between operations  0.66 us (2%)
  local copies, waits for them, and re-layouts  0.6 us (2%)
    pallas_call x1, Pallas kernels, local(): pl.pallas_call(functools.partial(kernel, (n_src, n_space, count)), out_sh...  36.6 us

profile of v7, /device:TPU:1, one launch (start us, length us, event | category | flops | bytes accessed | tf_op | source)
XLA Modules:
  0.0 37.8 jit_solution(9002618534487055186)
XLA Ops:
  0.7 36.6 %shard_map.109 = f32[8,128]{1,0:T(8,128)S(1)} custom-call(f32[8,96,128]{2,1,0:T(8,128)} %bitcast.12, f32[8,96,128]{2,1,0:T(8,128)} %bitcast.13, f32[2,128]{1,0:T(2,128)} %log_sigma.1, f32[2,128]{1,0:T(2,128)} %charge.1, f32[2,128]{1,0:T(2,128)} %log_tau.1, f32[2,128]{1,0:T(2,128)} %exponent.1, s32[2,128]{1,0:T(2,128)} %active_in.1, s32[1]{0:T(128)S(6)} %copy.15.source_group, ...), custom_call_target="tpu_custom_call" | custom-call | tf_op jit(solution)/shard_map/pallas_call | solution.py:554
  37.2 0.6 %copy.16 = f32[4,2,128]{2,1,0:T(2,128)} copy(f32[4,2,128]{2,1,0:T(2,128)S(1)} %bitcast.11) | data formatting | bytes 8192
